TPU v7x, 256 devices: a whole 4x4x8 slice. The times are simulated.
256 devices in a mesh: dp: 2 (over x_hi), gx: 16 (over z, core), gy: 8 (over y, x_lo).
Axes of the slice: x: 4 (x_hi: 2, x_lo: 2; x = x_hi * 2 + x_lo), y: 4, z: 8, core: 2. Of those that a mesh axis runs over, the one named last changes fastest.
Arguments:
- activations: bfloat16 [2, 32, 64, 128, 128], P('dp', None, 'gx', 'gy'), may hold values from -6 to 6
- kernel: bfloat16 [64, 32, 3, 3, 3], replicated, may hold values from -0.21875 to 0.21875
- out_grad: bfloat16 [2, 64, 64, 128, 128], P('dp', None, 'gx', 'gy'), may hold values from -6 to 6
Outputs:
- output: bfloat16 [2, 64, 64, 128, 128], P('dp', None, 'gx', 'gy')
- in_grad: bfloat16 [2, 32, 64, 128, 128], P('dp', None, 'gx', 'gy')
- kernel_grad: float32 [64, 32, 3, 3, 3], replicated
All inputs are finite; a program needn't handle non-finite values.
Results may differ from a plain program's by a relative error of at most 0.0014.
Values may be sent and summed in bfloat16 or wider, within the bound.
A program may use at most 64 MiB of HBM per device.

v0:
```python
import math

import jax
import jax.numpy as jnp
from jax import lax
from jax.sharding import PartitionSpec as P


def with_halo(cells, sides, width):
    for axis, dim in sides:
        count = lax.axis_size(axis)
        head = lax.slice_in_dim(cells, 0, width, axis=dim)
        tail = lax.slice_in_dim(cells, cells.shape[dim] - width, cells.shape[dim], axis=dim)
        cells = jnp.concatenate(
            [
                lax.ppermute(tail, axis, [(i, (i + 1) % count) for i in range(count)]),
                cells,
                lax.ppermute(head, axis, [((i + 1) % count, i) for i in range(count)]),
            ],
            axis=dim,
        )
    return cells


def wrap_depth(field):
    return jnp.concatenate([field[..., -1:], field, field[..., :1]], axis=4)


def forward_conv(padded, weights):
    return lax.conv_general_dilated(
        padded,
        weights,
        (1, 1, 1),
        "VALID",
        dimension_numbers=("NCDHW", "OIDHW", "NCDHW"),
        preferred_element_type=jnp.float32,
    )


def weight_conv(padded, cotangent):
    return lax.conv_general_dilated(
        padded,
        cotangent,
        (1, 1, 1),
        "VALID",
        dimension_numbers=("CNDHW", "IODHW", "CNDHW"),
        preferred_element_type=jnp.float32,
    )


def local(activations, kernel, out_grad):
    act_ext = with_halo(activations, (("gx", 2), ("gy", 3)), 1)
    grad_ext = with_halo(out_grad, (("gx", 2), ("gy", 3)), 1)
    act_pad = wrap_depth(act_ext)
    output = forward_conv(act_pad, kernel).astype(jnp.bfloat16)
    flipped = jnp.flip(kernel, (2, 3, 4)).transpose(1, 0, 2, 3, 4)
    in_grad = forward_conv(wrap_depth(grad_ext), flipped).astype(jnp.bfloat16)
    local_term = weight_conv(act_pad, out_grad)
    summed = lax.psum(local_term, ("dp", "gx", "gy"))
    shape_now = activations.shape
    total = (
        shape_now[0]
        * lax.axis_size("dp")
        * shape_now[2]
        * lax.axis_size("gx")
        * shape_now[3]
        * lax.axis_size("gy")
        * shape_now[4]
    )
    kernel_grad = summed * jnp.float32(1.0 / math.sqrt(total))
    return (output, in_grad, kernel_grad)


def solution(mesh):
    return jax.shard_map(
        local,
        mesh=mesh,
        in_specs=(P("dp", None, "gx", "gy", None), P(), P("dp", None, "gx", "gy", None)),
        out_specs=(P("dp", None, "gx", "gy", None), P("dp", None, "gx", "gy", None), P()),
        check_vma=False,
    )
```

profile of v0, /device:TPU:1, one launch (start us, length us, event | category | flops | bytes accessed | tf_op | source)
XLA Modules:
  0.0 450.2 jit_solution(17937101851074039768)
XLA Ops:
  8.3 3.0 collective-permute-start
  11.6 1.7 collective-permute-done
  21.3 2.0 collective-permute-start.5
  23.3 4.8 %copy.38 = bf16[1,64,4,16,128]{1,0,4,3,2:T(2,128)(2,1)} copy(bf16[1,64,4,16,128]{4,3,2,1,0:T(8,128)(2,1)S(1)} %copy-done.2) | data formatting | bytes 2097152 | tf_op args[2]
  28.1 2.4 collective-permute-start.3
  34.6 1.7 pad
  36.3 9.6 %reshape.8 = bf16[32,6,18,1,8,17]{5,4,0,2,1,3:T(8,128)(2,1)} reshape(bf16[32,6,18,1,136]{4,0,3,2,1:T(8,128)(2,1)} %pad) | data formatting | bytes 1880064 | tf_op jit(solution)/shard_map/conv_general_dilated | solution.py:30
  45.9 10.3 %copy.28 = bf16[32,6,18,1,8,17]{0,4,5,2,1,3:T(8,128)(2,1)} copy(bf16[32,6,18,1,8,17]{5,4,0,2,1,3:T(8,128)(2,1)} %reshape.8) | data formatting | bytes 1880064 | tf_op jit(solution)/shard_map/conv_general_dilated | solution.py:30
  57.3 9.2 %select_convert_fusion.1 = bf16[4,16,8,17,64]{4,2,3,1,0:T(8,128)(2,1)S(1)} fusion(pred[8,17]{0,1:T(8,128)(4,1)S(1)} %copy-done.4, bf16[64,32,3,3,3]{0,1,4,3,2:T(8,128)(2,1)S(1)} %copy-done, bf16[32,6,18,1,7,2]{0,4,5,2,1,3:T(8,128)(2,1)S(1)} %slice.56, bf16[32,6,18,1,8,17]{0,4,5,2,1,3:T(8,128)(2,1)} %copy.28), kind=kOutput, calls=%fused_computation.5 | convolution fusion | flops 966858752 | bytes 2261640 | tf_op jit(solution)/shard_map/conv_general_dilated | solution.py:30
  66.6 1.7 copy.29
  68.3 13.0 %copy.37 = bf16[1,32,6,18,130]{1,0,4,3,2:T(2,128)(2,1)} copy(bf16[1,32,6,18,130]{4,1,3,2,0:T(8,128)(2,1)S(1)} %pad_maximum_fusion) | data formatting | bytes 1797120 | tf_op jit(solution)/shard_map/concatenate | solution.py:26
  81.3 52.5 %fusion.34 = f32[64,32,3,3,3]{0,1,4,3,2:T(8,128)} fusion(bf16[1,32,6,18,130]{1,0,4,3,2:T(2,128)(2,1)} %copy.37, bf16[1,64,4,16,128]{1,0,4,3,2:T(2,128)(2,1)} %copy.38), kind=kOutput, calls=%fused_computation.47 | convolution fusion | flops 905969664 | bytes 2168320 | tf_op jit(solution)/shard_map/conv_general_dilated | solution.py:41
  133.9 1.7 slice_bitcast_fusion.1
  135.5 4.6 %copy.39 = bf16[1,64,4,16,128]{4,3,2,1,0:T(8,128)(2,1)} copy(bf16[1,64,4,16,128]{1,3,4,2,0:T(8,128)(2,1)} %slice_bitcast_fusion.1) | data formatting | bytes 2097152
  142.9 4.0 collective-permute-start.7
  146.9 247.3 %all-reduce.2.cloned.1.call-done = f32[64,32,3,3,3]{0,1,4,3,2:T(8,128)} async-done(((f32[64,32,3,3,3]{0,1,4,3,2:T(8,128)}), f32[64,32,3,3,3]{0,1,4,3,2:T(8,128)}) %all-reduce.2.cloned.1.call-update) | async-done | bytes 221200 | tf_op jit(solution)/shard_map/psum | solution.py:59
  394.2 1.8 broadcast_multiply_fusion
  397.1 4.6 %maximum_bitcast_fusion = bf16[64,6,18,1,130]{4,0,2,1,3:T(8,128)(2,1)} fusion(bf16[1,64,6,18,1]{4,1,3,2,0:T(8,128)(2,1)S(1)} %get-tuple-element.10, bf16[1,64,6,1,128]{4,1,3,2,0:T(8,128)(2,1)S(1)} %collective-permute-done.7, bf16[1,64,6,16,128]{4,1,3,2,0:T(8,128)(2,1)S(1)} %constant_dynamic-update-slice_fusion.3, ...), kind=kLoop, calls=%fused_computation.18 | loop fusion | flops 8985600 | bytes 3594240 | tf_op jit(solution)/shard_map/concatenate | solution.py:26
  401.6 6.2 %copy.41 = bf16[64,6,18,1,130]{0,4,2,1,3:T(8,128)(2,1)} copy(bf16[64,6,18,1,130]{4,0,2,1,3:T(8,128)(2,1)} %maximum_bitcast_fusion) | data formatting | bytes 3594240
  407.9 4.7 %pad.2.clone = bf16[64,6,18,1,136]{0,4,2,1,3:T(8,128)(2,1)} pad(bf16[64,6,18,1,130]{0,4,2,1,3:T(8,128)(2,1)} %copy.41, bf16[]{:T(256)} %constant.4), padding=0_0x0_0x0_0x0_0x0_6 | pad | bytes 3677186 | tf_op jit(solution)/shard_map/concatenate | solution.py:26
  412.5 7.7 %reshape.15 = bf16[64,6,18,1,8,17]{0,5,4,2,1,3:T(8,128)(2,1)} reshape(bf16[64,6,18,1,136]{0,4,2,1,3:T(8,128)(2,1)} %pad.2.clone) | data formatting | bytes 3760128 | tf_op jit(solution)/shard_map/conv_general_dilated | solution.py:30
  420.3 3.2 copy.35
  423.6 15.9 %select_convert_fusion = bf16[4,16,8,17,32]{4,2,3,1,0:T(8,128)(2,1)S(1)} fusion(pred[8,17]{0,1:T(8,128)(4,1)S(1)} %copy-done.5, bf16[64,32,3,3,3]{0,1,4,3,2:T(8,128)(2,1)S(1)} %copy-done, bf16[64,6,18,1,7,2]{0,4,5,2,1,3:T(8,128)(2,1)S(1)} %slice.64, bf16[64,6,18,1,8,17]{0,4,5,2,1,3:T(8,128)(2,1)S(1)} %copy.35), kind=kOutput, calls=%fused_computation.4 | convolution fusion | flops 969453568 | bytes 2741384 | tf_op jit(solution)/shard_map/conv_general_dilated | solution.py:30
  440.2 2.9 copy.40
  (49 shorter events, 19.1 us)
Async XLA Ops:
  7.2 50.1 %copy-start = (bf16[64,32,3,3,3]{0,1,4,3,2:T(8,128)(2,1)S(1)}, bf16[64,32,3,3,3]{0,1,4,3,2:T(8,128)(2,1)}, u32[]{:S(2)}) copy-start(bf16[64,32,3,3,3]{0,1,4,3,2:T(8,128)(2,1)} %param.4) | copy-start | bytes 331780
  7.2 16.1 %copy-start.2 = (bf16[1,64,4,16,128]{4,3,2,1,0:T(8,128)(2,1)S(1)}, bf16[1,64,4,16,128]{4,3,2,1,0:T(8,128)(2,1)}, u32[]{:S(2)}) copy-start(bf16[1,64,4,16,128]{4,3,2,1,0:T(8,128)(2,1)} %param.5) | copy-start | bytes 3145732
  7.2 387.0 %all-reduce.2.cloned.1.call-start = ((), (), s32[]{:S(2)}) async-start(), calls=%async_computation | async-start | bytes 884736 | tf_op jit(solution)/shard_map/psum | solution.py:59
  8.3 5.0 %collective-permute-start = (bf16[1,32,1,16,128]{4,3,2,1,0:T(8,128)(2,1)S(1)}, bf16[1,32,1,16,128]{4,3,2,1,0:T(8,128)(2,1)S(1)}, u32[]{:S(2)}, u32[]{:S(2)}) collective-permute-start(bf16[1,32,1,16,128]{4,3,2,1,0:T(8,128)(2,1)S(1)} %get-tuple-element.20), channel_id=1, source_target_pairs={{0,8},{8,16},{16,24},{24,32},{32,40},{40,48},{48,56},{56,64},{64,7... | collective-permute-start | bytes 393224 | tf_op jit(solution)/shard_map/ppermute | solution.py:16
  11.4 4.7 %collective-permute-start.1 = (bf16[1,32,1,16,128]{4,3,2,1,0:T(8,128)(2,1)S(1)}, bf16[1,32,1,16,128]{4,3,2,1,0:T(8,128)(2,1)S(1)}, u32[]{:S(2)}, u32[]{:S(2)}) collective-permute-start(bf16[1,32,1,16,128]{4,3,2,1,0:T(8,128)(2,1)S(1)} %get-tuple-element.19), channel_id=1, source_target_pairs={{8,0},{16,8},{24,16},{32,24},{40,32},{48,40},{56,48},{64,56},{72,6... | collective-permute-start | bytes 393224 | tf_op jit(solution)/shard_map/ppermute | solution.py:18
  16.2 14.3 %collective-permute-start.2 = (bf16[1,32,6,1,128]{4,3,2,1,0:T(2,128)(2,1)S(1)}, bf16[1,32,6,1,128]{4,3,2,1,0:T(2,128)(2,1)S(1)}, u32[]{:S(2)}, u32[]{:S(2)}) collective-permute-start(bf16[1,32,6,1,128]{4,3,2,1,0:T(2,128)(2,1)S(1)} %get-tuple-element.18), channel_id=1, source_target_pairs={{0,1},{1,2},{2,3},{3,4},{4,5},{5,6},{6,7},{7,0},{8,9},{9,10},{10,1... | collective-permute-start | bytes 147464 | tf_op jit(solution)/shard_map/ppermute | solution.py:16
  19.4 120.8 %collective-permute-start.4 = (bf16[1,64,1,16,128]{4,1,3,2,0:T(8,128)(2,1)}, bf16[1,64,1,16,128]{4,1,3,2,0:T(8,128)(2,1)}, u32[]{:S(2)}, u32[]{:S(2)}) collective-permute-start(bf16[1,64,1,16,128]{4,1,3,2,0:T(8,128)(2,1)} %copy.46), channel_id=1, source_target_pairs={{0,8},{8,16},{16,24},{24,32},{32,40},{40,48},{48,56},{56,64},{64,7... | collective-permute-start | bytes 786440 | tf_op jit(solution)/shard_map/ppermute | solution.py:16
  21.3 120.6 %collective-permute-start.5 = (bf16[1,64,1,16,128]{4,1,3,2,0:T(8,128)(2,1)}, bf16[1,64,1,16,128]{4,1,3,2,0:T(8,128)(2,1)}, u32[]{:S(2)}, u32[]{:S(2)}) collective-permute-start(bf16[1,64,1,16,128]{4,1,3,2,0:T(8,128)(2,1)} %copy.47), channel_id=1, source_target_pairs={{8,0},{16,8},{24,16},{32,24},{40,32},{48,40},{56,48},{64,56},{72,6... | collective-permute-start | bytes 786440 | tf_op jit(solution)/shard_map/ppermute | solution.py:18
  28.1 4.0 collective-permute-start.3
  45.9 11.4 %copy-start.4 = (pred[8,17]{0,1:T(8,128)(4,1)S(1)}, pred[8,17]{0,1:T(8,128)(4,1)}, u32[]{:S(2)}) copy-start(pred[8,17]{0,1:T(8,128)(4,1)} %constant.12) | copy-start | bytes 412
  81.3 52.5 %copy-start.1 = (bf16[4,16,8,17,64]{4,1,3,2,0:T(8,128)(2,1)S(1)}, bf16[4,16,8,17,64]{4,1,3,2,0:T(8,128)(2,1)}, u32[]{:S(2)}) copy-start(bf16[4,16,8,17,64]{4,1,3,2,0:T(8,128)(2,1)} %copy.29) | copy-start | bytes 3342340
  133.9 7.3 %copy-start.3 = (bf16[1,64,4,16,128]{4,3,2,1,0:T(8,128)(2,1)S(1)}, bf16[1,64,4,16,128]{4,3,2,1,0:T(8,128)(2,1)}, u32[]{:S(2)}) copy-start(bf16[1,64,4,16,128]{4,3,2,1,0:T(8,128)(2,1)} %param.5) | copy-start | bytes 3145732
  142.9 253.1 %collective-permute-start.7 = (bf16[1,64,6,1,128]{4,1,3,2,0:T(8,128)(2,1)S(1)}, bf16[1,64,6,1,128]{4,1,3,2,0:T(8,128)(2,1)S(1)}, u32[]{:S(2)}, u32[]{:S(2)}) collective-permute-start(bf16[1,64,6,1,128]{4,1,3,2,0:T(8,128)(2,1)S(1)} %get-tuple-element.12), channel_id=1, source_target_pairs={{1,0},{2,1},{3,2},{4,3},{5,4},{6,5},{7,6},{0,7},{9,8},{10,9},{11,1... | collective-permute-start | bytes 294920 | tf_op jit(solution)/shard_map/ppermute | solution.py:18
  146.9 249.1 %collective-permute-start.6 = (bf16[1,64,6,1,128]{4,1,3,2,0:T(8,128)(2,1)S(1)}, bf16[1,64,6,1,128]{4,1,3,2,0:T(8,128)(2,1)S(1)}, u32[]{:S(2)}, u32[]{:S(2)}) collective-permute-start(bf16[1,64,6,1,128]{4,1,3,2,0:T(8,128)(2,1)S(1)} %get-tuple-element.11), channel_id=1, source_target_pairs={{0,1},{1,2},{2,3},{3,4},{4,5},{5,6},{6,7},{7,0},{8,9},{9,10},{10,1... | collective-permute-start | bytes 294920 | tf_op jit(solution)/shard_map/ppermute | solution.py:16
  420.2 3.3 copy-start.5
Sparse Core Ops, SparseCore 0:
  140.3 253.9 all-reduce.1
where the time goes:
time: 456 us; the launch traced here: 450 us
  waiting for transfers between devices  252 us (55%)
  local copies, waits for them, and re-layouts  83.3 us (18%)
  matrix products  77.7 us (17%)
  between operations  14.5 us (3%)
  starting transfers between devices  14.2 us (3%)
  other arithmetic  8.67 us (2%)
    psum x1, waiting for transfers between devices, local(): summed = lax.psum(local_term, ('dp', 'gx', 'gy'))  247 us
    conv_general_dilated x1, matrix products, weight_conv(): lax.conv_general_dilated(padded, cotangent, (1, 1, 1), 'VALID', dimension...  52.5 us
    conv_general_dilated x6, local copies, waits for them, and re-layouts, forward_conv(): lax.conv_general_dilated(padded, weights, (1, 1, 1), 'VALID', dimension_n...  32 us
    conv_general_dilated x2, matrix products, forward_conv(): lax.conv_general_dilated(padded, weights, (1, 1, 1), 'VALID', dimension_n...  25.1 us
    unnamed x24, local copies, waits for them, and re-layouts  23.2 us
    concatenate x3, local copies, waits for them, and re-layouts, wrap_depth(): return jnp.concatenate([field[..., -1:], field, field[..., :1]], axis=4)  19.4 us
  transfers between devices with their start and end apart: 9, of which 4 were waited for; matrix products, arithmetic and copies ran while one was open for 27% of the time, Pallas kernels for 0%

commit v1 on v0

v1 whole, which is shorter than its diff:
```python
import functools
import math

import jax
import jax.numpy as jnp
from jax import lax
from jax.experimental import pallas as pl
from jax.experimental.pallas import tpu as pltpu
from jax.sharding import PartitionSpec as P

MESH = pl.DeviceIdType.MESH
LANES = 128
AROUND = [(-1, 0), (1, 0), (0, -1), (0, 1), (-1, -1), (-1, 1), (1, -1), (1, 1)]


def kernel(sizes, scale, act_hbm, w_ref, og_hbm, out_hbm, ing_hbm, kg_ref,
           act_v, og_v, act_e, og_e, og_r, stage, w_fwd, w_bwd, grad, dense, slots, near, sums, zed, gathered, full,
           out_v, ing_v, in_sem, out_sem, ha_send, ha_recv, ho_send, ho_recv,
           p1_send, p1_recv, p2_send, p2_recv, p3_send, p3_recv, p4_send, p4_recv, p5_send, p5_recv):
    n_dp, n_gx, n_gy = sizes
    cin, ni, nj, _ = act_v.shape
    cout = og_v.shape[0]
    nz = n_gx // 2
    group = n_dp * n_gy
    dp, gx, gy = lax.axis_index("dp"), lax.axis_index("gx"), lax.axis_index("gy")
    z, core = lax.div(gx, 2), lax.rem(gx, 2)
    place = dp * n_gy + gy

    def shifted(di, dj):
        return (dp, lax.rem(gx + di + n_gx, n_gx), lax.rem(gy + dj + n_gy, n_gy))

    def along_z(dz):
        return (dp, lax.rem(z + dz, nz) * 2 + core, gy)

    other_core = (dp, z * 2 + 1 - core, gy)

    def across(d):
        peer = lax.rem(place + d, group)
        return (lax.div(peer, n_gy), gx, lax.rem(peer, n_gy))

    act_in = pltpu.make_async_copy(act_hbm, act_v, in_sem.at[0])
    og_in = pltpu.make_async_copy(og_hbm, og_v, in_sem.at[1])
    act_in.start()
    og_in.start()

    barrier = pltpu.get_barrier_semaphore()

    def greet(target):
        pl.semaphore_signal(barrier, inc=1, device_id=target, device_id_type=MESH)

    for di, dj in AROUND:
        if di:
            greet(shifted(di, dj))
    lax.fori_loop(1, nz, lambda d, c: (greet(along_z(d)), c)[1], 0)
    lax.fori_loop(1, group, lambda d, c: (greet(across(d)), c)[1], 0)

    def halo(field, n, send, recv):
        di, dj = AROUND[n]
        rows = {-1: (1, ni + 1, 1), 0: (1, 1, ni), 1: (ni, 0, 1)}[di]
        cols = {-1: (1, nj + 1, 1), 0: (1, 1, nj), 1: (nj, 0, 1)}[dj]
        return pltpu.make_async_remote_copy(
            src_ref=field.at[pl.ds(rows[0], rows[2]), :, pl.ds(cols[0] * LANES, cols[2] * LANES)],
            dst_ref=field.at[pl.ds(rows[1], rows[2]), :, pl.ds(cols[1] * LANES, cols[2] * LANES)],
            send_sem=send.at[n],
            recv_sem=recv.at[n],
            device_id=shifted(di, dj),
            device_id_type=MESH,
        )

    act_in.wait()

    def turn_act(i, carry):
        stage[pl.ds(0, cin * nj)] = act_v[:, i].astype(jnp.float32).reshape(cin * nj, LANES)
        for j in range(nj):
            act_e[i + 1, :, pl.ds((j + 1) * LANES, LANES)] = stage[pl.ds(j, cin, stride=nj)].astype(jnp.bfloat16)
        return carry

    lax.fori_loop(0, ni, turn_act, 0)
    pl.semaphore_wait(barrier, 6 + (nz - 1) + (group - 1))
    for n in range(8):
        halo(act_e, n, ha_send, ha_recv).start()

    og_in.wait()

    def turn_og(i, carry):
        stage[...] = og_v[:, i].astype(jnp.float32).reshape(cout * nj, LANES)
        for j in range(nj):
            rows = stage[pl.ds(j, cout, stride=nj)]
            at = pl.ds(j * LANES, LANES)
            og_e[i + 1, :, pl.ds((j + 1) * LANES, LANES)] = rows.astype(jnp.bfloat16)
            og_r[i, pl.ds(0, cout), at] = pltpu.roll(rows, LANES - 1, 1).astype(jnp.bfloat16)
            og_r[i, pl.ds(cout, cout), at] = rows.astype(jnp.bfloat16)
            og_r[i, pl.ds(2 * cout, cout), at] = pltpu.roll(rows, 1, 1).astype(jnp.bfloat16)
        return carry

    lax.fori_loop(0, ni, turn_og, 0)
    for n in range(8):
        halo(og_e, n, ho_send, ho_recv).start()

    w = w_ref[...].astype(jnp.float32).reshape(9, 3, cin, cout)
    by_tap = jnp.concatenate([w[:, e].reshape(9 * cin, cout) for e in range(3)], axis=1)
    w_fwd[...] = by_tap.T.astype(jnp.bfloat16)
    w_bwd[...] = jnp.concatenate([w[n].reshape(3 * cin, cout) for n in range(9)], axis=1).astype(jnp.bfloat16)

    for n in range(8):
        halo(act_e, n, ha_send, ha_recv).wait_recv()

    grad[...] = jnp.zeros_like(grad)

    def weight_term(i, carry):
        taps = jnp.concatenate(
            [act_e[i + a, :, pl.ds(b * LANES, nj * LANES)] for a in range(3) for b in range(3)], axis=0
        )
        grad[...] += lax.dot_general(taps, og_r[i], (((1,), (1,)), ((), ())), preferred_element_type=jnp.float32)
        return carry

    lax.fori_loop(0, ni, weight_term, 0)
    tall = 9 * cin
    half = tall // 2
    dense[pl.ds(0, tall)] = grad[:, :LANES]
    dense[pl.ds(tall, half)] = jnp.concatenate([grad[:half, LANES:], grad[half:, LANES:]], axis=1)
    part = slots.shape[2]
    for s in range(n_gx):
        slots[s // nz, s % nz] = dense[pl.ds(s * part, part)]

    def forward(i):
        def chunk(p, carry):
            taps = jnp.concatenate(
                [
                    act_e[i + a, :, pl.ds(pl.multiple_of((2 * p + b) * LANES, LANES), 2 * LANES)]
                    for a in range(3)
                    for b in range(3)
                ],
                axis=0,
            )
            y = jnp.dot(w_fwd[...], taps, preferred_element_type=jnp.float32)
            for q in range(2):
                t = y[:, q * LANES : (q + 1) * LANES]
                total = t[cout : 2 * cout] + pltpu.roll(t[:cout], 1, 1) + pltpu.roll(t[2 * cout :], LANES - 1, 1)
                stage[pl.ds(2 * p + q, cout, stride=nj)] = total
            return carry

        lax.fori_loop(0, nj // 2, chunk, 0)
        out_v[i] = stage[...].astype(jnp.bfloat16).reshape(cout, nj, LANES)
        pltpu.make_async_copy(out_v.at[i], out_hbm.at[:, i], out_sem.at[i]).start()

    def backward(i):
        def chunk(p, carry):
            taps = jnp.concatenate(
                [
                    og_e[i + 2 - a, :, pl.ds(pl.multiple_of((2 * p + 2 - b) * LANES, LANES), 2 * LANES)]
                    for a in range(3)
                    for b in range(3)
                ],
                axis=0,
            )
            y = jnp.dot(w_bwd[...], taps, preferred_element_type=jnp.float32)
            for q in range(2):
                t = y[:, q * LANES : (q + 1) * LANES]
                total = t[cin : 2 * cin] + pltpu.roll(t[:cin], LANES - 1, 1) + pltpu.roll(t[2 * cin :], 1, 1)
                stage[pl.ds(2 * p + q, cin, stride=nj)] = total
            return carry

        lax.fori_loop(0, nj // 2, chunk, 0)
        ing_v[i] = stage[pl.ds(0, cin * nj)].astype(jnp.bfloat16).reshape(cin, nj, LANES)
        pltpu.make_async_copy(ing_v.at[i], ing_hbm.at[:, i], out_sem.at[ni + i]).start()

    def far_first(t):
        return nz // 2 + lax.div(t + 1, 2) * (1 - 2 * lax.rem(t, 2))

    def to_core(dz):
        at = lax.rem(z + dz, nz)
        return pltpu.make_async_remote_copy(
            src_ref=slots.at[1 - core, at], dst_ref=near.at[at], send_sem=p1_send.at[dz], recv_sem=p1_recv.at[dz],
            device_id=other_core, device_id_type=MESH)

    def to_z(dz):
        return pltpu.make_async_remote_copy(
            src_ref=sums.at[dz], dst_ref=zed.at[dz], send_sem=p2_send.at[dz], recv_sem=p2_recv.at[dz],
            device_id=along_z(dz), device_id_type=MESH)

    def to_group(d):
        return pltpu.make_async_remote_copy(
            src_ref=gathered.at[place], dst_ref=gathered.at[place], send_sem=p3_send.at[d], recv_sem=p3_recv.at[d],
            device_id=across(d), device_id_type=MESH)

    def back_z(dz):
        return pltpu.make_async_remote_copy(
            src_ref=full.at[core, z], dst_ref=full.at[core, z], send_sem=p4_send.at[dz], recv_sem=p4_recv.at[dz],
            device_id=along_z(dz), device_id_type=MESH)

    def back_core(dz):
        at = lax.rem(z - dz + nz, nz)
        return pltpu.make_async_remote_copy(
            src_ref=full.at[core, at], dst_ref=full.at[core, at], send_sem=p5_send.at[dz], recv_sem=p5_recv.at[dz],
            device_id=other_core, device_id_type=MESH)

    def each(low, high, do):
        def body(t, carry):
            do(t)
            return carry

        lax.fori_loop(low, high, body, 0)

    each(0, nz, lambda t: to_core(far_first(t)).start())
    each(0, 1, forward)

    def pass_z(t):
        dz = far_first(t)
        to_core(dz).wait_recv()
        at = lax.rem(z + dz, nz)
        sums[dz] = slots[core, at] + near[at]

    def send_z(t):
        pass_z(t)
        to_z(far_first(t)).start()

    each(0, nz - 1, send_z)
    pass_z(nz - 1)
    each(1, 3, forward)
    each(1, nz, lambda dz: to_z(dz).wait_recv())
    total = sums[0]
    for dz in range(1, nz):
        total = total + zed[dz]
    gathered[place] = total
    each(1, group, lambda d: to_group(d).start())
    each(3, ni, forward)
    for n in range(8):
        halo(og_e, n, ho_send, ho_recv).wait_recv()
    each(0, 1, backward)
    each(1, group, lambda d: to_group(d).wait_recv())
    total = gathered[0]
    for p in range(1, group):
        total = total + gathered[p]
    full[core, z] = total * jnp.float32(scale)
    each(1, nz, lambda dz: back_z(dz).start())
    back_core(0).start()
    each(1, 3, backward)

    def forward_core(t):
        dz = t + 1
        back_z(dz).wait_recv()
        back_core(dz).start()

    each(0, nz - 1, forward_core)
    each(3, ni, backward)

    each(0, nz, lambda dz: back_core(dz).wait_recv())
    for s in range(n_gx):
        dense[pl.ds(s * part, part)] = full[s // nz, s % nz]
    for n in range(9):
        rows = pl.ds(n * cin, cin)
        kg_ref[pl.ds(n * 3 * cin, cin)] = dense[rows, pl.ds(0, cout)]
        kg_ref[pl.ds((n * 3 + 1) * cin, cin)] = dense[rows, pl.ds(cout, cout)]
    third = jnp.concatenate([dense[pl.ds(tall, half), :cout], dense[pl.ds(tall, half), cout:]], axis=0)
    for n in range(9):
        kg_ref[pl.ds((n * 3 + 2) * cin, cin)] = third[n * cin : (n + 1) * cin]

    for n in range(8):
        halo(act_e, n, ha_send, ha_recv).wait_send()
        halo(og_e, n, ho_send, ho_recv).wait_send()
    each(0, nz, lambda dz: to_core(dz).wait_send())
    each(1, nz, lambda dz: to_z(dz).wait_send())
    each(1, group, lambda d: to_group(d).wait_send())
    each(1, nz, lambda dz: back_z(dz).wait_send())
    each(0, nz, lambda dz: back_core(dz).wait_send())
    each(0, ni, lambda i: pltpu.make_async_copy(out_v.at[i], out_hbm.at[:, i], out_sem.at[i]).wait())
    each(0, ni, lambda i: pltpu.make_async_copy(ing_v.at[i], ing_hbm.at[:, i], out_sem.at[ni + i]).wait())


def local(sizes, activations, weights, out_grad):
    n_dp, n_gx, n_gy = sizes
    univ, cin, ni, nj, nk = activations.shape
    cout = out_grad.shape[1]
    nz, group = n_gx // 2, n_dp * n_gy
    scale = 1.0 / math.sqrt(univ * n_dp * ni * n_gx * nj * n_gy * nk)
    part = 27 * cin * cout // (LANES * n_gx)
    bf16, f32 = jnp.bfloat16, jnp.float32
    dma = pltpu.SemaphoreType.DMA
    taps = weights.transpose(2, 3, 4, 1, 0).reshape(27 * cin, cout)
    output, in_grad, kernel_grad = pl.pallas_call(
        functools.partial(kernel, sizes, scale),
        out_shape=(
            jax.ShapeDtypeStruct((cout, ni, nj, nk), bf16),
            jax.ShapeDtypeStruct((cin, ni, nj, nk), bf16),
            jax.ShapeDtypeStruct((27 * cin, cout), f32),
        ),
        in_specs=[
            pl.BlockSpec(memory_space=pl.ANY),
            pl.BlockSpec(memory_space=pltpu.VMEM),
            pl.BlockSpec(memory_space=pl.ANY),
        ],
        out_specs=(
            pl.BlockSpec(memory_space=pl.ANY),
            pl.BlockSpec(memory_space=pl.ANY),
            pl.BlockSpec(memory_space=pltpu.VMEM),
        ),
        scratch_shapes=[
            pltpu.VMEM((cin, ni, nj, nk), bf16),
            pltpu.VMEM((cout, ni, nj, nk), bf16),
            pltpu.VMEM((ni + 2, cin, (nj + 2) * nk), bf16),
            pltpu.VMEM((ni + 2, cout, (nj + 2) * nk), bf16),
            pltpu.VMEM((ni, 3 * cout, nj * nk), bf16),
            pltpu.VMEM((cout * nj, nk), f32),
            pltpu.VMEM((3 * cout, 9 * cin), bf16),
            pltpu.VMEM((3 * cin, 9 * cout), bf16),
            pltpu.VMEM((9 * cin, 3 * cout), f32),
            pltpu.VMEM((part * n_gx, LANES), f32),
            pltpu.VMEM((2, nz, part, LANES), f32),
            pltpu.VMEM((nz, part, LANES), f32),
            pltpu.VMEM((nz, part, LANES), f32),
            pltpu.VMEM((nz, part, LANES), f32),
            pltpu.VMEM((group, part, LANES), f32),
            pltpu.VMEM((2, nz, part, LANES), f32),
            pltpu.VMEM((ni, cout, nj, nk), bf16),
            pltpu.VMEM((ni, cin, nj, nk), bf16),
            dma((2,)),
            dma((2 * ni,)),
            dma((8,)), dma((8,)), dma((8,)), dma((8,)),
            dma((nz,)), dma((nz,)), dma((nz,)), dma((nz,)),
            dma((group,)), dma((group,)),
            dma((nz,)), dma((nz,)), dma((nz,)), dma((nz,)),
        ],
        compiler_params=pltpu.CompilerParams(
            collective_id=0, has_side_effects=True, vmem_limit_bytes=48 * 1024 * 1024
        ),
        cost_estimate=pl.CostEstimate(flops=3_000_000_000, bytes_accessed=4_000_000, transcendentals=0),
    )(activations[0], taps, out_grad[0])
    kernel_grad = kernel_grad.reshape(3, 3, 3, cin, cout).transpose(4, 3, 0, 1, 2)
    return (output[None], in_grad[None], kernel_grad)


def solution(mesh):
    sizes = (mesh.shape["dp"], mesh.shape["gx"], mesh.shape["gy"])
    return jax.shard_map(
        functools.partial(local, sizes),
        mesh=mesh,
        in_specs=(P("dp", None, "gx", "gy", None), P(), P("dp", None, "gx", "gy", None)),
        out_specs=(P("dp", None, "gx", "gy", None), P("dp", None, "gx", "gy", None), P()),
        check_vma=False,
    )
```

time: 456 us -> 46.3 us (0.10); the launches traced: 450 us -> 45.9 us
  waiting for transfers between devices: 252 us -> 0 us
  matrix products: 77.7 us -> 0 us
  local copies, waits for them, and re-layouts: 83.3 us -> 5.72 us
  Pallas kernels: 0 us -> 39.5 us
  starting transfers between devices: 14.2 us -> 0 us
  between operations: 14.5 us -> 0.65 us
  other arithmetic: 8.67 us -> 0 us
    psum x1 -> x0, waiting for transfers between devices: 247 us -> none  [local(): summed = lax.psum(local_term, ('dp', 'gx', 'gy'))]
    conv_general_dilated x3 -> x0, matrix products: 77.7 us -> none  [the longest x1 52.5 us: weight_conv(): lax.conv_general_dilated(padded, cotangent, (1, 1, 1), 'VALID', dimension...]
    pallas_call x0 -> x1, Pallas kernels: none -> 39.5 us  [local(): pl.pallas_call(functools.partial(kernel, sizes, scale), out_shape=(jax.Sh...]
    conv_general_dilated x6 -> x0, local copies, waits for them, and re-layouts: 32 us -> none  [forward_conv(): lax.conv_general_dilated(padded, weights, (1, 1, 1), 'VALID', dimension_n...]
    concatenate x6 -> x0, local copies, waits for them, and re-layouts: 20.4 us -> none  [the longest x3 19.4 us: wrap_depth(): return jnp.concatenate([field[..., -1:], field, field[..., :1]], axis=4)]
    unnamed x24 -> x9, local copies, waits for them, and re-layouts: 23.2 us -> 5.72 us
    ppermute x8 -> x0, starting transfers between devices: 14.1 us -> none  [the longest x4 8.66 us: with_halo(): lax.ppermute(head, axis, [((i + 1) % count, i) for i in range(count)])]
    concatenate x4 -> x0, other arithmetic: 6.85 us -> none  [the longest x3 6.63 us: wrap_depth(): return jnp.concatenate([field[..., -1:], field, field[..., :1]], axis=4)]
  transfers between devices with their start and end apart: 9 -> 0, of which waited for: 4 -> 0; matrix products, arithmetic and copies ran while one was open for 27% -> 0% of each run, Pallas kernels for 0% -> 0%
where the time goes in v1:
time: 46.3 us; the launch traced here: 45.9 us
  Pallas kernels  39.5 us (85%)
  local copies, waits for them, and re-layouts  5.72 us (12%)
  between operations  0.65 us (1%)
    pallas_call x1, Pallas kernels, local(): pl.pallas_call(functools.partial(kernel, sizes, scale), out_shape=(jax.Sh...  39.5 us
    unnamed x9, local copies, waits for them, and re-layouts  5.72 us

profile of v1, /device:TPU:1, one launch (start us, length us, event | category | flops | bytes accessed | tf_op | source)
XLA Modules:
  0.0 45.9 jit_solution(17361535255447069551)
XLA Ops:
  0.6 0.0 copy-start
  0.6 1.2 %copy-done = bf16[1,64,4,16,128]{4,3,2,1,0:T(8,128)(2,1)S(1)} copy-done((bf16[1,64,4,16,128]{4,3,2,1,0:T(8,128)(2,1)S(1)}, bf16[1,64,4,16,128]{4,3,2,1,0:T(8,128)(2,1)}, u32[]{:S(2)}) %copy-start) | copy-done | bytes 1048600
  1.9 0.0 copy-start.1
  1.9 1.0 %copy-done.1 = bf16[1,32,4,16,128]{4,3,2,1,0:T(8,128)(2,1)S(1)} copy-done((bf16[1,32,4,16,128]{4,3,2,1,0:T(8,128)(2,1)S(1)}, bf16[1,32,4,16,128]{4,3,2,1,0:T(8,128)(2,1)}, u32[]{:S(2)}) %copy-start.1) | copy-done | bytes 524312
  2.9 0.0 copy-start.2
  2.9 0.9 %copy-done.2 = bf16[64,32,3,3,3]{0,1,4,3,2:T(8,128)(2,1)S(1)} copy-done((bf16[64,32,3,3,3]{0,1,4,3,2:T(8,128)(2,1)S(1)}, bf16[64,32,3,3,3]{0,1,4,3,2:T(8,128)(2,1)}, u32[]{:S(2)}) %copy-start.2) | copy-done | bytes 110616
  3.8 39.5 %shard_map.58 = (bf16[64,4,16,128]{3,2,1,0:T(8,128)(2,1)S(1)}, bf16[32,4,16,128]{3,2,1,0:T(8,128)(2,1)S(1)}, f32[864,64]{1,0:T(8,128)S(1)}) custom-call(bf16[32,4,16,128]{3,2,1,0:T(8,128)(2,1)S(1)} %bitcast.14, bf16[864,64]{1,0:T(8,128)(2,1)S(1)} %bitcast.15, bf16[64,4,16,128]{3,2,1,0:T(8,128)(2,1)S(1)} %bitcast.13), custom_call_target="tpu_custom_call" | custom-call | flops 3000000000 | bytes 4000000 | tf_op jit(solution)/shard_map/pallas_call | solution.py:281
  43.4 1.0 %copy.9 = bf16[1,64,4,16,128]{4,3,2,1,0:T(8,128)(2,1)} copy(bf16[1,64,4,16,128]{4,3,2,1,0:T(8,128)(2,1)S(1)} %bitcast.10) | data formatting | bytes 2097152
  44.3 0.8 %copy.10 = bf16[1,32,4,16,128]{4,3,2,1,0:T(8,128)(2,1)} copy(bf16[1,32,4,16,128]{4,3,2,1,0:T(8,128)(2,1)S(1)} %bitcast.11) | data formatting | bytes 1048576
  45.1 0.8 %copy.11 = f32[64,32,3,3,3]{0,1,4,3,2:T(8,128)} copy(f32[64,32,3,3,3]{0,1,4,3,2:T(8,128)S(1)} %bitcast.12) | data formatting | bytes 442368
Async XLA Ops:
  0.6 1.2 %copy-start = (bf16[1,64,4,16,128]{4,3,2,1,0:T(8,128)(2,1)S(1)}, bf16[1,64,4,16,128]{4,3,2,1,0:T(8,128)(2,1)}, u32[]{:S(2)}) copy-start(bf16[1,64,4,16,128]{4,3,2,1,0:T(8,128)(2,1)} %param.5) | copy-start | bytes 3145732
  1.9 1.0 %copy-start.1 = (bf16[1,32,4,16,128]{4,3,2,1,0:T(8,128)(2,1)S(1)}, bf16[1,32,4,16,128]{4,3,2,1,0:T(8,128)(2,1)}, u32[]{:S(2)}) copy-start(bf16[1,32,4,16,128]{4,3,2,1,0:T(8,128)(2,1)} %param.3) | copy-start | bytes 1572868
  2.9 0.9 %copy-start.2 = (bf16[64,32,3,3,3]{0,1,4,3,2:T(8,128)(2,1)S(1)}, bf16[64,32,3,3,3]{0,1,4,3,2:T(8,128)(2,1)}, u32[]{:S(2)}) copy-start(bf16[64,32,3,3,3]{0,1,4,3,2:T(8,128)(2,1)} %param.4) | copy-start | bytes 331780

commit v2 on v1

--- a/solution.py
+++ b/solution.py
@@ -13,8 +13,8 @@
 AROUND = [(-1, 0), (1, 0), (0, -1), (0, 1), (-1, -1), (-1, 1), (1, -1), (1, 1)]
 
 
-def kernel(sizes, scale, act_hbm, w_ref, og_hbm, out_hbm, ing_hbm, kg_ref,
-           act_v, og_v, act_e, og_e, og_r, stage, w_fwd, w_bwd, grad, dense, slots, near, sums, zed, gathered, full,
+def kernel(sizes, scale, act_hbm, w_hbm, og_hbm, out_hbm, ing_hbm, kg_ref,
+           act_v, w_v, og_v, act_e, og_e, og_r, stage, w_fwd, w_bwd, grad, dense, slots, near, sums, parts, lifted, full,
            out_v, ing_v, in_sem, out_sem, ha_send, ha_recv, ho_send, ho_recv,
            p1_send, p1_recv, p2_send, p2_recv, p3_send, p3_recv, p4_send, p4_recv, p5_send, p5_recv):
     n_dp, n_gx, n_gy = sizes
@@ -38,11 +38,6 @@
         peer = lax.rem(place + d, group)
         return (lax.div(peer, n_gy), gx, lax.rem(peer, n_gy))
 
-    act_in = pltpu.make_async_copy(act_hbm, act_v, in_sem.at[0])
-    og_in = pltpu.make_async_copy(og_hbm, og_v, in_sem.at[1])
-    act_in.start()
-    og_in.start()
-
     barrier = pltpu.get_barrier_semaphore()
 
     def greet(target):
@@ -53,6 +48,13 @@
             greet(shifted(di, dj))
     lax.fori_loop(1, nz, lambda d, c: (greet(along_z(d)), c)[1], 0)
     lax.fori_loop(1, group, lambda d, c: (greet(across(d)), c)[1], 0)
+
+    act_in = pltpu.make_async_copy(act_hbm, act_v, in_sem.at[0])
+    og_in = pltpu.make_async_copy(og_hbm, og_v, in_sem.at[1])
+    w_in = pltpu.make_async_copy(w_hbm, w_v, in_sem.at[2])
+    act_in.start()
+    og_in.start()
+    w_in.start()
 
     def halo(field, n, send, recv):
         di, dj = AROUND[n]
@@ -97,7 +99,8 @@
     for n in range(8):
         halo(og_e, n, ho_send, ho_recv).start()
 
-    w = w_ref[...].astype(jnp.float32).reshape(9, 3, cin, cout)
+    w_in.wait()
+    w = w_v[...].astype(jnp.float32).reshape(9, 3, cin, cout)
     by_tap = jnp.concatenate([w[:, e].reshape(9 * cin, cout) for e in range(3)], axis=1)
     w_fwd[...] = by_tap.T.astype(jnp.bfloat16)
     w_bwd[...] = jnp.concatenate([w[n].reshape(3 * cin, cout) for n in range(9)], axis=1).astype(jnp.bfloat16)
@@ -120,14 +123,17 @@
     dense[pl.ds(0, tall)] = grad[:, :LANES]
     dense[pl.ds(tall, half)] = jnp.concatenate([grad[:half, LANES:], grad[half:, LANES:]], axis=1)
     part = slots.shape[2]
-    for s in range(n_gx):
-        slots[s // nz, s % nz] = dense[pl.ds(s * part, part)]
+    extra = 2 * group * part - tall - half
+    if extra:
+        dense[pl.ds(tall + half, extra)] = jnp.zeros((extra, LANES), jnp.float32)
+    for s in range(2 * group):
+        slots[s // group, s % group] = dense[pl.ds(s * part, part)]
 
     def forward(i):
-        def chunk(p, carry):
+        for p in range(nj // 2):
             taps = jnp.concatenate(
                 [
-                    act_e[i + a, :, pl.ds(pl.multiple_of((2 * p + b) * LANES, LANES), 2 * LANES)]
+                    act_e[i + a, :, pl.ds((2 * p + b) * LANES, 2 * LANES)]
                     for a in range(3)
                     for b in range(3)
                 ],
@@ -138,17 +144,14 @@
                 t = y[:, q * LANES : (q + 1) * LANES]
                 total = t[cout : 2 * cout] + pltpu.roll(t[:cout], 1, 1) + pltpu.roll(t[2 * cout :], LANES - 1, 1)
                 stage[pl.ds(2 * p + q, cout, stride=nj)] = total
-            return carry
-
-        lax.fori_loop(0, nj // 2, chunk, 0)
         out_v[i] = stage[...].astype(jnp.bfloat16).reshape(cout, nj, LANES)
         pltpu.make_async_copy(out_v.at[i], out_hbm.at[:, i], out_sem.at[i]).start()
 
     def backward(i):
-        def chunk(p, carry):
+        for p in range(nj // 2):
             taps = jnp.concatenate(
                 [
-                    og_e[i + 2 - a, :, pl.ds(pl.multiple_of((2 * p + 2 - b) * LANES, LANES), 2 * LANES)]
+                    og_e[i + 2 - a, :, pl.ds((2 * p + 2 - b) * LANES, 2 * LANES)]
                     for a in range(3)
                     for b in range(3)
                 ],
@@ -159,40 +162,33 @@
                 t = y[:, q * LANES : (q + 1) * LANES]
                 total = t[cin : 2 * cin] + pltpu.roll(t[:cin], LANES - 1, 1) + pltpu.roll(t[2 * cin :], 1, 1)
                 stage[pl.ds(2 * p + q, cin, stride=nj)] = total
-            return carry
-
-        lax.fori_loop(0, nj // 2, chunk, 0)
         ing_v[i] = stage[pl.ds(0, cin * nj)].astype(jnp.bfloat16).reshape(cin, nj, LANES)
         pltpu.make_async_copy(ing_v.at[i], ing_hbm.at[:, i], out_sem.at[ni + i]).start()
 
-    def far_first(t):
-        return nz // 2 + lax.div(t + 1, 2) * (1 - 2 * lax.rem(t, 2))
-
-    def to_core(dz):
-        at = lax.rem(z + dz, nz)
-        return pltpu.make_async_remote_copy(
-            src_ref=slots.at[1 - core, at], dst_ref=near.at[at], send_sem=p1_send.at[dz], recv_sem=p1_recv.at[dz],
+    def to_core():
+        return pltpu.make_async_remote_copy(
+            src_ref=slots.at[1 - core], dst_ref=near, send_sem=p1_send.at[0], recv_sem=p1_recv.at[0],
             device_id=other_core, device_id_type=MESH)
 
+    def to_group(d):
+        return pltpu.make_async_remote_copy(
+            src_ref=sums.at[lax.rem(place + d, group)], dst_ref=parts.at[place],
+            send_sem=p2_send.at[d], recv_sem=p2_recv.at[d], device_id=across(d), device_id_type=MESH)
+
     def to_z(dz):
         return pltpu.make_async_remote_copy(
-            src_ref=sums.at[dz], dst_ref=zed.at[dz], send_sem=p2_send.at[dz], recv_sem=p2_recv.at[dz],
+            src_ref=lifted.at[z], dst_ref=lifted.at[z], send_sem=p3_send.at[dz], recv_sem=p3_recv.at[dz],
             device_id=along_z(dz), device_id_type=MESH)
 
-    def to_group(d):
-        return pltpu.make_async_remote_copy(
-            src_ref=gathered.at[place], dst_ref=gathered.at[place], send_sem=p3_send.at[d], recv_sem=p3_recv.at[d],
+    def back_group(d):
+        return pltpu.make_async_remote_copy(
+            src_ref=full.at[core, place], dst_ref=full.at[core, place], send_sem=p4_send.at[d], recv_sem=p4_recv.at[d],
             device_id=across(d), device_id_type=MESH)
 
-    def back_z(dz):
-        return pltpu.make_async_remote_copy(
-            src_ref=full.at[core, z], dst_ref=full.at[core, z], send_sem=p4_send.at[dz], recv_sem=p4_recv.at[dz],
-            device_id=along_z(dz), device_id_type=MESH)
-
-    def back_core(dz):
-        at = lax.rem(z - dz + nz, nz)
-        return pltpu.make_async_remote_copy(
-            src_ref=full.at[core, at], dst_ref=full.at[core, at], send_sem=p5_send.at[dz], recv_sem=p5_recv.at[dz],
+    def back_core(d):
+        at = lax.rem(place - d + group, group)
+        return pltpu.make_async_remote_copy(
+            src_ref=full.at[core, at], dst_ref=full.at[core, at], send_sem=p5_send.at[d], recv_sem=p5_recv.at[d],
             device_id=other_core, device_id_type=MESH)
 
     def each(low, high, do):
@@ -202,52 +198,33 @@
 
         lax.fori_loop(low, high, body, 0)
 
-    each(0, nz, lambda t: to_core(far_first(t)).start())
-    each(0, 1, forward)
-
-    def pass_z(t):
-        dz = far_first(t)
-        to_core(dz).wait_recv()
-        at = lax.rem(z + dz, nz)
-        sums[dz] = slots[core, at] + near[at]
-
-    def send_z(t):
-        pass_z(t)
-        to_z(far_first(t)).start()
-
-    each(0, nz - 1, send_z)
-    pass_z(nz - 1)
-    each(1, 3, forward)
+    to_core().start()
+    to_core().wait_recv()
+    sums[...] = slots[core] + near[...]
+    each(1, group, lambda d: to_group(d).start())
+    parts[place] = sums[place]
+    each(0, 2, forward)
+    each(1, group, lambda d: to_group(d).wait_recv())
+    lifted[z] = jnp.sum(parts[...], axis=0)
+    each(1, nz, lambda dz: to_z(dz).start())
+    each(2, ni, forward)
     each(1, nz, lambda dz: to_z(dz).wait_recv())
-    total = sums[0]
-    for dz in range(1, nz):
-        total = total + zed[dz]
-    gathered[place] = total
-    each(1, group, lambda d: to_group(d).start())
-    each(3, ni, forward)
+    full[core, place] = jnp.sum(lifted[...], axis=0) * jnp.float32(scale)
+    each(1, group, lambda d: back_group(d).start())
+    back_core(0).start()
     for n in range(8):
         halo(og_e, n, ho_send, ho_recv).wait_recv()
-    each(0, 1, backward)
-    each(1, group, lambda d: to_group(d).wait_recv())
-    total = gathered[0]
-    for p in range(1, group):
-        total = total + gathered[p]
-    full[core, z] = total * jnp.float32(scale)
-    each(1, nz, lambda dz: back_z(dz).start())
-    back_core(0).start()
-    each(1, 3, backward)
+    each(0, ni, backward)
 
     def forward_core(t):
-        dz = t + 1
-        back_z(dz).wait_recv()
-        back_core(dz).start()
-
-    each(0, nz - 1, forward_core)
-    each(3, ni, backward)
-
-    each(0, nz, lambda dz: back_core(dz).wait_recv())
-    for s in range(n_gx):
-        dense[pl.ds(s * part, part)] = full[s // nz, s % nz]
+        d = t + 1
+        back_group(d).wait_recv()
+        back_core(d).start()
+
+    each(0, group - 1, forward_core)
+    each(0, group, lambda d: back_core(d).wait_recv())
+    for s in range(2 * group):
+        dense[pl.ds(s * part, part)] = full[s // group, s % group]
     for n in range(9):
         rows = pl.ds(n * cin, cin)
         kg_ref[pl.ds(n * 3 * cin, cin)] = dense[rows, pl.ds(0, cout)]
@@ -259,11 +236,11 @@
     for n in range(8):
         halo(act_e, n, ha_send, ha_recv).wait_send()
         halo(og_e, n, ho_send, ho_recv).wait_send()
-    each(0, nz, lambda dz: to_core(dz).wait_send())
+    to_core().wait_send()
+    each(1, group, lambda d: to_group(d).wait_send())
     each(1, nz, lambda dz: to_z(dz).wait_send())
-    each(1, group, lambda d: to_group(d).wait_send())
-    each(1, nz, lambda dz: back_z(dz).wait_send())
-    each(0, nz, lambda dz: back_core(dz).wait_send())
+    each(1, group, lambda d: back_group(d).wait_send())
+    each(0, group, lambda d: back_core(d).wait_send())
     each(0, ni, lambda i: pltpu.make_async_copy(out_v.at[i], out_hbm.at[:, i], out_sem.at[i]).wait())
     each(0, ni, lambda i: pltpu.make_async_copy(ing_v.at[i], ing_hbm.at[:, i], out_sem.at[ni + i]).wait())
 
@@ -274,7 +251,7 @@
     cout = out_grad.shape[1]
     nz, group = n_gx // 2, n_dp * n_gy
     scale = 1.0 / math.sqrt(univ * n_dp * ni * n_gx * nj * n_gy * nk)
-    part = 27 * cin * cout // (LANES * n_gx)
+    part = -(-27 * cin * cout // (LANES * 2 * group))
     bf16, f32 = jnp.bfloat16, jnp.float32
     dma = pltpu.SemaphoreType.DMA
     taps = weights.transpose(2, 3, 4, 1, 0).reshape(27 * cin, cout)
@@ -286,9 +263,9 @@
             jax.ShapeDtypeStruct((27 * cin, cout), f32),
         ),
         in_specs=[
-            pl.BlockSpec(memory_space=pl.ANY),
-            pl.BlockSpec(memory_space=pltpu.VMEM),
-            pl.BlockSpec(memory_space=pl.ANY),
+            pl.BlockSpec(memory_space=pltpu.HBM),
+            pl.BlockSpec(memory_space=pltpu.HBM),
+            pl.BlockSpec(memory_space=pltpu.HBM),
         ],
         out_specs=(
             pl.BlockSpec(memory_space=pl.ANY),
@@ -297,6 +274,7 @@
         ),
         scratch_shapes=[
             pltpu.VMEM((cin, ni, nj, nk), bf16),
+            pltpu.VMEM((27 * cin, cout), bf16),
             pltpu.VMEM((cout, ni, nj, nk), bf16),
             pltpu.VMEM((ni + 2, cin, (nj + 2) * nk), bf16),
             pltpu.VMEM((ni + 2, cout, (nj + 2) * nk), bf16),
@@ -305,27 +283,29 @@
             pltpu.VMEM((3 * cout, 9 * cin), bf16),
             pltpu.VMEM((3 * cin, 9 * cout), bf16),
             pltpu.VMEM((9 * cin, 3 * cout), f32),
-            pltpu.VMEM((part * n_gx, LANES), f32),
-            pltpu.VMEM((2, nz, part, LANES), f32),
+            pltpu.VMEM((2 * group * part, LANES), f32),
+            pltpu.VMEM((2, group, part, LANES), f32),
+            pltpu.VMEM((group, part, LANES), f32),
+            pltpu.VMEM((group, part, LANES), f32),
+            pltpu.VMEM((group, part, LANES), f32),
             pltpu.VMEM((nz, part, LANES), f32),
-            pltpu.VMEM((nz, part, LANES), f32),
-            pltpu.VMEM((nz, part, LANES), f32),
-            pltpu.VMEM((group, part, LANES), f32),
-            pltpu.VMEM((2, nz, part, LANES), f32),
+            pltpu.VMEM((2, group, part, LANES), f32),
             pltpu.VMEM((ni, cout, nj, nk), bf16),
             pltpu.VMEM((ni, cin, nj, nk), bf16),
-            dma((2,)),
+            dma((3,)),
             dma((2 * ni,)),
             dma((8,)), dma((8,)), dma((8,)), dma((8,)),
-            dma((nz,)), dma((nz,)), dma((nz,)), dma((nz,)),
+            dma((1,)), dma((1,)),
             dma((group,)), dma((group,)),
-            dma((nz,)), dma((nz,)), dma((nz,)), dma((nz,)),
+            dma((nz,)), dma((nz,)),
+            dma((group,)), dma((group,)),
+            dma((group,)), dma((group,)),
         ],
         compiler_params=pltpu.CompilerParams(
             collective_id=0, has_side_effects=True, vmem_limit_bytes=48 * 1024 * 1024
         ),
         cost_estimate=pl.CostEstimate(flops=3_000_000_000, bytes_accessed=4_000_000, transcendentals=0),
-    )(activations[0], taps, out_grad[0])
+    )(*(pltpu.with_memory_space_constraint(x, pltpu.HBM) for x in (activations[0], taps, out_grad[0])))
     kernel_grad = kernel_grad.reshape(3, 3, 3, cin, cout).transpose(4, 3, 0, 1, 2)
     return (output[None], in_grad[None], kernel_grad)
 

time: 46.3 us -> 40.2 us (0.87)
  local copies, waits for them, and re-layouts: 5.72 us -> 2.53 us
  Pallas kernels: 39.5 us -> 37 us
    unnamed x9 -> x3, local copies, waits for them, and re-layouts: 5.72 us -> 2.53 us
    pallas_call x1, Pallas kernels: 39.5 us -> 37 us  [local(): pl.pallas_call(functools.partial(kernel, sizes, scale), out_shape=(jax.Sh...]
where the time goes in v2:
time: 40.2 us; the launch traced here: 40.1 us
  Pallas kernels  37 us (92%)
  local copies, waits for them, and re-layouts  2.53 us (6%)
  between operations  0.64 us (2%)
    pallas_call x1, Pallas kernels, local(): pl.pallas_call(functools.partial(kernel, sizes, scale), out_shape=(jax.Sh...  37 us
    unnamed x3, local copies, waits for them, and re-layouts  2.53 us

profile of v2, /device:TPU:1, one launch (start us, length us, event | category | flops | bytes accessed | tf_op | source)
XLA Modules:
  0.0 40.1 jit_solution(2716816200273273512)
XLA Ops:
  0.6 37.0 %shard_map.58 = (bf16[64,4,16,128]{3,2,1,0:T(8,128)(2,1)S(1)}, bf16[32,4,16,128]{3,2,1,0:T(8,128)(2,1)S(1)}, f32[864,64]{1,0:T(8,128)S(1)}) custom-call(bf16[32,4,16,128]{3,2,1,0:T(8,128)(2,1)} %bitcast.14, bf16[864,64]{1,0:T(8,128)(2,1)} %bitcast.15, bf16[64,4,16,128]{3,2,1,0:T(8,128)(2,1)} %bitcast.13), custom_call_target="tpu_custom_call" | custom-call | flops 3000000000 | bytes 4000000 | tf_op jit(solution)/shard_map/pallas_call | solution.py:258
  37.6 1.0 %copy.9 = bf16[1,64,4,16,128]{4,3,2,1,0:T(8,128)(2,1)} copy(bf16[1,64,4,16,128]{4,3,2,1,0:T(8,128)(2,1)S(1)} %bitcast.10) | data formatting | bytes 2097152
  38.6 0.8 %copy.10 = bf16[1,32,4,16,128]{4,3,2,1,0:T(8,128)(2,1)} copy(bf16[1,32,4,16,128]{4,3,2,1,0:T(8,128)(2,1)S(1)} %bitcast.11) | data formatting | bytes 1048576
  39.4 0.8 %copy.11 = f32[64,32,3,3,3]{0,1,4,3,2:T(8,128)} copy(f32[64,32,3,3,3]{0,1,4,3,2:T(8,128)S(1)} %bitcast.12) | data formatting | bytes 442368

commit v3 on v2

--- a/solution.py
+++ b/solution.py
@@ -14,7 +14,7 @@
 
 
 def kernel(sizes, scale, act_hbm, w_hbm, og_hbm, out_hbm, ing_hbm, kg_ref,
-           act_v, w_v, og_v, act_e, og_e, og_r, stage, w_fwd, w_bwd, grad, dense, slots, near, sums, parts, lifted, full,
+           act_v, w_v, og_v, act_e, og_e, og_r, land_x, land_y, land_c, stage, w_fwd, w_bwd, grad, dense, slots, near, sums, parts, lifted, full,
            out_v, ing_v, in_sem, out_sem, ha_send, ha_recv, ho_send, ho_recv,
            p1_send, p1_recv, p2_send, p2_recv, p3_send, p3_recv, p4_send, p4_recv, p5_send, p5_recv):
     n_dp, n_gx, n_gy = sizes
@@ -35,8 +35,13 @@
     other_core = (dp, z * 2 + 1 - core, gy)
 
     def across(d):
-        peer = lax.rem(place + d, group)
-        return (lax.div(peer, n_gy), gx, lax.rem(peer, n_gy))
+        return (lax.rem(dp + lax.div(d, n_gy), n_dp), gx, lax.rem(gy + lax.rem(d, n_gy), n_gy))
+
+    def place_across(d):
+        return lax.rem(dp + lax.div(d, n_gy), n_dp) * n_gy + lax.rem(gy + lax.rem(d, n_gy), n_gy)
+
+    def source_across(d):
+        return lax.rem(dp - lax.div(d, n_gy) + n_dp, n_dp) * n_gy + lax.rem(gy - lax.rem(d, n_gy) + n_gy, n_gy)
 
     barrier = pltpu.get_barrier_semaphore()
 
@@ -44,10 +49,10 @@
         pl.semaphore_signal(barrier, inc=1, device_id=target, device_id_type=MESH)
 
     for di, dj in AROUND:
-        if di:
-            greet(shifted(di, dj))
+        greet(shifted(di, dj))
+    lax.fori_loop(2, n_gy - 1, lambda d, c: (greet(across(d)), c)[1], 0)
+    lax.fori_loop(n_gy, group, lambda d, c: (greet(across(d)), c)[1], 0)
     lax.fori_loop(1, nz, lambda d, c: (greet(along_z(d)), c)[1], 0)
-    lax.fori_loop(1, group, lambda d, c: (greet(across(d)), c)[1], 0)
 
     act_in = pltpu.make_async_copy(act_hbm, act_v, in_sem.at[0])
     og_in = pltpu.make_async_copy(og_hbm, og_v, in_sem.at[1])
@@ -56,19 +61,34 @@
     og_in.start()
     w_in.start()
 
-    def halo(field, n, send, recv):
+    def halo(field, n, send, recv, landing=None):
         di, dj = AROUND[n]
         rows = {-1: (1, ni + 1, 1), 0: (1, 1, ni), 1: (ni, 0, 1)}[di]
         cols = {-1: (1, nj + 1, 1), 0: (1, 1, nj), 1: (nj, 0, 1)}[dj]
+        if landing is None:
+            landing = field.at[pl.ds(rows[1], rows[2]), :, pl.ds(cols[1] * LANES, cols[2] * LANES)]
         return pltpu.make_async_remote_copy(
             src_ref=field.at[pl.ds(rows[0], rows[2]), :, pl.ds(cols[0] * LANES, cols[2] * LANES)],
-            dst_ref=field.at[pl.ds(rows[1], rows[2]), :, pl.ds(cols[1] * LANES, cols[2] * LANES)],
+            dst_ref=landing,
             send_sem=send.at[n],
             recv_sem=recv.at[n],
             device_id=shifted(di, dj),
             device_id_type=MESH,
         )
 
+    def act_halo(n):
+        if n < 2:
+            landing = land_x.at[pl.ds(n, 1)]
+        elif n < 4:
+            landing = land_y.at[n - 2]
+        else:
+            landing = land_c.at[pl.ds(n - 4, 1)]
+        return halo(act_e, n, ha_send, ha_recv, landing)
+
+    act_e[0] = jnp.zeros_like(act_e[0])
+    act_e[ni + 1] = jnp.zeros_like(act_e[0])
+    for edge in (0, nj + 1):
+        act_e[pl.ds(1, ni), :, pl.ds(edge * LANES, LANES)] = jnp.zeros((ni, cin, LANES), jnp.bfloat16)
     act_in.wait()
 
     def turn_act(i, carry):
@@ -79,8 +99,8 @@
 
     lax.fori_loop(0, ni, turn_act, 0)
     pl.semaphore_wait(barrier, 6 + (nz - 1) + (group - 1))
-    for n in range(8):
-        halo(act_e, n, ha_send, ha_recv).start()
+    for n in (2, 3, 0, 1, 4, 5, 6, 7):
+        act_halo(n).start()
 
     og_in.wait()
 
@@ -96,28 +116,47 @@
         return carry
 
     lax.fori_loop(0, ni, turn_og, 0)
-    for n in range(8):
-        halo(og_e, n, ho_send, ho_recv).start()
-
-    w_in.wait()
-    w = w_v[...].astype(jnp.float32).reshape(9, 3, cin, cout)
-    by_tap = jnp.concatenate([w[:, e].reshape(9 * cin, cout) for e in range(3)], axis=1)
-    w_fwd[...] = by_tap.T.astype(jnp.bfloat16)
-    w_bwd[...] = jnp.concatenate([w[n].reshape(3 * cin, cout) for n in range(9)], axis=1).astype(jnp.bfloat16)
-
-    for n in range(8):
-        halo(act_e, n, ha_send, ha_recv).wait_recv()
-
-    grad[...] = jnp.zeros_like(grad)
-
-    def weight_term(i, carry):
+
+    def product(taps, cells):
+        return lax.dot_general(taps, cells, (((1,), (1,)), ((), ())), preferred_element_type=jnp.float32)
+
+    def weight_term(i):
         taps = jnp.concatenate(
             [act_e[i + a, :, pl.ds(b * LANES, nj * LANES)] for a in range(3) for b in range(3)], axis=0
         )
-        grad[...] += lax.dot_general(taps, og_r[i], (((1,), (1,)), ((), ())), preferred_element_type=jnp.float32)
-        return carry
-
-    lax.fori_loop(0, ni, weight_term, 0)
+        return product(taps, og_r[i])
+
+    grad[...] = weight_term(0)
+    for i in range(1, ni):
+        grad[...] += weight_term(i)
+
+    for n in range(2):
+        act_halo(n).wait_recv()
+    act_e[ni + 1, :, pl.ds(LANES, nj * LANES)] = land_x[0]
+    act_e[0, :, pl.ds(LANES, nj * LANES)] = land_x[1]
+    for a, outer, inner in ((0, 0, 0), (2, ni + 1, ni - 1)):
+        taps = jnp.concatenate([act_e[outer, :, pl.ds(b * LANES, nj * LANES)] for b in range(3)], axis=0)
+        grad[pl.ds(a * 3 * cin, 3 * cin)] += product(taps, og_r[inner])
+    for n in range(2, 4):
+        act_halo(n).wait_recv()
+    act_e[pl.ds(1, ni), :, pl.ds((nj + 1) * LANES, LANES)] = land_y[0]
+    act_e[pl.ds(1, ni), :, pl.ds(0, LANES)] = land_y[1]
+    for n in range(4, 8):
+        act_halo(n).wait_recv()
+        di, dj = AROUND[n]
+        act_e[ni + 1 if di < 0 else 0, :, pl.ds((nj + 1 if dj < 0 else 0) * LANES, LANES)] = land_c[n - 4]
+    for b, outer, inner in ((0, 0, 0), (2, nj + 1, nj - 1)):
+        taps = jnp.concatenate(
+            [
+                jnp.concatenate([act_e[i + a, :, pl.ds(outer * LANES, LANES)] for i in range(ni)], axis=1)
+                for a in range(3)
+            ],
+            axis=0,
+        )
+        cells = jnp.concatenate([og_r[i, :, pl.ds(inner * LANES, LANES)] for i in range(ni)], axis=1)
+        term = product(taps, cells)
+        for a in range(3):
+            grad[pl.ds((3 * a + b) * cin, cin)] += term[a * cin : (a + 1) * cin]
     tall = 9 * cin
     half = tall // 2
     dense[pl.ds(0, tall)] = grad[:, :LANES]
@@ -172,7 +211,7 @@
 
     def to_group(d):
         return pltpu.make_async_remote_copy(
-            src_ref=sums.at[lax.rem(place + d, group)], dst_ref=parts.at[place],
+            src_ref=sums.at[place_across(d)], dst_ref=parts.at[place],
             send_sem=p2_send.at[d], recv_sem=p2_recv.at[d], device_id=across(d), device_id_type=MESH)
 
     def to_z(dz):
@@ -186,7 +225,7 @@
             device_id=across(d), device_id_type=MESH)
 
     def back_core(d):
-        at = lax.rem(place - d + group, group)
+        at = source_across(d)
         return pltpu.make_async_remote_copy(
             src_ref=full.at[core, at], dst_ref=full.at[core, at], send_sem=p5_send.at[d], recv_sem=p5_recv.at[d],
             device_id=other_core, device_id_type=MESH)
@@ -199,14 +238,23 @@
         lax.fori_loop(low, high, body, 0)
 
     to_core().start()
+    w_in.wait()
+    w = w_v[...].astype(jnp.float32).reshape(9, 3, cin, cout)
+    by_tap = jnp.concatenate([w[:, e].reshape(9 * cin, cout) for e in range(3)], axis=1)
+    w_fwd[...] = by_tap.T.astype(jnp.bfloat16)
+    w_bwd[...] = jnp.concatenate([w[n].reshape(3 * cin, cout) for n in range(9)], axis=1).astype(jnp.bfloat16)
     to_core().wait_recv()
     sums[...] = slots[core] + near[...]
-    each(1, group, lambda d: to_group(d).start())
+    each(1, group, lambda d: to_group(group - d).start())
+    for n in range(2):
+        halo(og_e, n, ho_send, ho_recv).start()
     parts[place] = sums[place]
     each(0, 2, forward)
     each(1, group, lambda d: to_group(d).wait_recv())
     lifted[z] = jnp.sum(parts[...], axis=0)
     each(1, nz, lambda dz: to_z(dz).start())
+    for n in range(2, 8):
+        halo(og_e, n, ho_send, ho_recv).start()
     each(2, ni, forward)
     each(1, nz, lambda dz: to_z(dz).wait_recv())
     full[core, place] = jnp.sum(lifted[...], axis=0) * jnp.float32(scale)
@@ -234,7 +282,7 @@
         kg_ref[pl.ds((n * 3 + 2) * cin, cin)] = third[n * cin : (n + 1) * cin]
 
     for n in range(8):
-        halo(act_e, n, ha_send, ha_recv).wait_send()
+        act_halo(n).wait_send()
         halo(og_e, n, ho_send, ho_recv).wait_send()
     to_core().wait_send()
     each(1, group, lambda d: to_group(d).wait_send())
@@ -243,6 +291,16 @@
     each(0, group, lambda d: back_core(d).wait_send())
     each(0, ni, lambda i: pltpu.make_async_copy(out_v.at[i], out_hbm.at[:, i], out_sem.at[i]).wait())
     each(0, ni, lambda i: pltpu.make_async_copy(ing_v.at[i], ing_hbm.at[:, i], out_sem.at[ni + i]).wait())
+
+
+def deliver(*refs):
+    count = len(refs) // 2
+    sem = refs[-1]
+    copies = [pltpu.make_async_copy(refs[n], refs[count + n], sem.at[n]) for n in range(count)]
+    for copy in copies:
+        copy.start()
+    for copy in copies:
+        copy.wait()
 
 
 def local(sizes, activations, weights, out_grad):
@@ -279,6 +337,9 @@
             pltpu.VMEM((ni + 2, cin, (nj + 2) * nk), bf16),
             pltpu.VMEM((ni + 2, cout, (nj + 2) * nk), bf16),
             pltpu.VMEM((ni, 3 * cout, nj * nk), bf16),
+            pltpu.VMEM((2, cin, nj * nk), bf16),
+            pltpu.VMEM((2, ni, cin, nk), bf16),
+            pltpu.VMEM((4, cin, nk), bf16),
             pltpu.VMEM((cout * nj, nk), f32),
             pltpu.VMEM((3 * cout, 9 * cin), bf16),
             pltpu.VMEM((3 * cin, 9 * cout), bf16),
@@ -306,6 +367,14 @@
         ),
         cost_estimate=pl.CostEstimate(flops=3_000_000_000, bytes_accessed=4_000_000, transcendentals=0),
     )(*(pltpu.with_memory_space_constraint(x, pltpu.HBM) for x in (activations[0], taps, out_grad[0])))
+    held = tuple(pltpu.with_memory_space_constraint(x, pltpu.VMEM) for x in (output, in_grad, kernel_grad))
+    output, in_grad, kernel_grad = pl.pallas_call(
+        deliver,
+        out_shape=tuple(jax.ShapeDtypeStruct(x.shape, x.dtype) for x in held),
+        in_specs=[pl.BlockSpec(memory_space=pltpu.VMEM)] * 3,
+        out_specs=(pl.BlockSpec(memory_space=pltpu.HBM),) * 3,
+        scratch_shapes=[dma((3,))],
+    )(*held)
     kernel_grad = kernel_grad.reshape(3, 3, 3, cin, cout).transpose(4, 3, 0, 1, 2)
     return (output[None], in_grad[None], kernel_grad)
 

time: 40.2 us -> 37.5 us (0.933)
  local copies, waits for them, and re-layouts: 2.53 us -> 0 us
    unnamed x3 -> x0, local copies, waits for them, and re-layouts: 2.53 us -> none
    pallas_call x1, Pallas kernels: 37 us -> 35.5 us  [local(): pl.pallas_call(functools.partial(kernel, sizes, scale), out_shape=(jax.Sh...]
    pallas_call x0 -> x1, Pallas kernels: none -> 1.31 us  [local(): pl.pallas_call(deliver, out_shape=tuple((jax.ShapeDtypeStruct(x.shape, x....]
where the time goes in v3:
time: 37.5 us; the launch traced here: 37.4 us
  Pallas kernels  36.8 us (98%)
  between operations  0.64 us (2%)
    pallas_call x1, Pallas kernels, local(): pl.pallas_call(functools.partial(kernel, sizes, scale), out_shape=(jax.Sh...  35.5 us
    pallas_call x1, Pallas kernels, local(): pl.pallas_call(deliver, out_shape=tuple((jax.ShapeDtypeStruct(x.shape, x....  1.31 us

profile of v3, /device:TPU:1, one launch (start us, length us, event | category | flops | bytes accessed | tf_op | source)
XLA Modules:
  0.0 37.4 jit_solution(10106924867612030870)
XLA Ops:
  0.6 35.5 %shard_map.58 = (bf16[64,4,16,128]{3,2,1,0:T(8,128)(2,1)S(1)}, bf16[32,4,16,128]{3,2,1,0:T(8,128)(2,1)S(1)}, f32[864,64]{1,0:T(8,128)S(1)}) custom-call(bf16[32,4,16,128]{3,2,1,0:T(8,128)(2,1)} %bitcast.12, bf16[864,64]{1,0:T(8,128)(2,1)} %bitcast.15, bf16[64,4,16,128]{3,2,1,0:T(8,128)(2,1)} %bitcast.10), custom_call_target="tpu_custom_call" | custom-call | flops 3000000000 | bytes 4000000 | tf_op jit(solution)/shard_map/pallas_call | solution.py:316
  36.1 1.3 %shard_map.59 = (bf16[64,4,16,128]{3,2,1,0:T(8,128)(2,1)}, bf16[32,4,16,128]{3,2,1,0:T(8,128)(2,1)}, f32[864,64]{1,0:T(8,128)}) custom-call(bf16[64,4,16,128]{3,2,1,0:T(8,128)(2,1)S(1)} %get-tuple-element.9.refs_0_, bf16[32,4,16,128]{3,2,1,0:T(8,128)(2,1)S(1)} %get-tuple-element.10.refs_1_, f32[864,64]{1,0:T(8,128)S(1)} %get-tuple-element.11.refs_2_), custom_call_target="tpu_custom_call" | custom-call | tf_op jit(solution)/shard_map/pallas_call | solution.py:371

commit v4 on v3

--- a/solution.py
+++ b/solution.py
@@ -13,10 +13,10 @@
 AROUND = [(-1, 0), (1, 0), (0, -1), (0, 1), (-1, -1), (-1, 1), (1, -1), (1, 1)]
 
 
-def kernel(sizes, scale, act_hbm, w_hbm, og_hbm, out_hbm, ing_hbm, kg_ref,
-           act_v, w_v, og_v, act_e, og_e, og_r, land_x, land_y, land_c, stage, w_fwd, w_bwd, grad, dense, slots, near, sums, parts, lifted, full,
+def kernel(sizes, scale, act_hbm, w_hbm, og_hbm, out_hbm, ing_hbm, full,
+           act_v, w_v, og_v, act_e, og_e, og_r, land_x, land_y, land_c, stage, w_fwd, w_bwd, grad, dense, slots, parts, lifted, mine,
            out_v, ing_v, in_sem, out_sem, ha_send, ha_recv, ho_send, ho_recv,
-           p1_send, p1_recv, p2_send, p2_recv, p3_send, p3_recv, p4_send, p4_recv, p5_send, p5_recv):
+           p1_send, p1_recv, p2_send, p2_recv, p3_send, p3_recv, mine_sem):
     n_dp, n_gx, n_gy = sizes
     cin, ni, nj, _ = act_v.shape
     cout = og_v.shape[0]
@@ -32,27 +32,15 @@
     def along_z(dz):
         return (dp, lax.rem(z + dz, nz) * 2 + core, gy)
 
-    other_core = (dp, z * 2 + 1 - core, gy)
-
-    def across(d):
-        return (lax.rem(dp + lax.div(d, n_gy), n_dp), gx, lax.rem(gy + lax.rem(d, n_gy), n_gy))
+    def across(d, flip=0):
+        return (
+            lax.rem(dp + lax.div(d, n_gy), n_dp),
+            z * 2 + core + flip * (1 - 2 * core),
+            lax.rem(gy + lax.rem(d, n_gy), n_gy),
+        )
 
     def place_across(d):
         return lax.rem(dp + lax.div(d, n_gy), n_dp) * n_gy + lax.rem(gy + lax.rem(d, n_gy), n_gy)
-
-    def source_across(d):
-        return lax.rem(dp - lax.div(d, n_gy) + n_dp, n_dp) * n_gy + lax.rem(gy - lax.rem(d, n_gy) + n_gy, n_gy)
-
-    barrier = pltpu.get_barrier_semaphore()
-
-    def greet(target):
-        pl.semaphore_signal(barrier, inc=1, device_id=target, device_id_type=MESH)
-
-    for di, dj in AROUND:
-        greet(shifted(di, dj))
-    lax.fori_loop(2, n_gy - 1, lambda d, c: (greet(across(d)), c)[1], 0)
-    lax.fori_loop(n_gy, group, lambda d, c: (greet(across(d)), c)[1], 0)
-    lax.fori_loop(1, nz, lambda d, c: (greet(along_z(d)), c)[1], 0)
 
     act_in = pltpu.make_async_copy(act_hbm, act_v, in_sem.at[0])
     og_in = pltpu.make_async_copy(og_hbm, og_v, in_sem.at[1])
@@ -60,6 +48,22 @@
     act_in.start()
     og_in.start()
     w_in.start()
+
+    barrier = pltpu.get_barrier_semaphore()
+
+    def greet(target):
+        pl.semaphore_signal(barrier, inc=1, device_id=target, device_id_type=MESH)
+
+    steps = [(d, flip) for d in range(2, group) for flip in range(2) if d not in (n_gy - 1,)]
+    hops = {}
+    for d, flip in steps:
+        far_x, far_y = 2 * (d // n_gy), d % n_gy
+        hops[d, flip] = min(far_y, n_gy - far_y) / 2 + (1.5 if far_y % 2 else far_x)
+    targets = [(hops[d, flip], across(d, flip)) for d, flip in steps]
+    targets += [(min(d, nz - d), along_z(d)) for d in range(1, nz)]
+    targets += [(abs(di) + 1.5 * abs(dj), shifted(di, dj)) for di, dj in AROUND]
+    for _, target in sorted(targets, key=lambda t: -t[0]):
+        greet(target)
 
     def halo(field, n, send, recv, landing=None):
         di, dj = AROUND[n]
@@ -98,7 +102,7 @@
         return carry
 
     lax.fori_loop(0, ni, turn_act, 0)
-    pl.semaphore_wait(barrier, 6 + (nz - 1) + (group - 1))
+    pl.semaphore_wait(barrier, 8 + 2 * (group - 3) + (nz - 1))
     for n in (2, 3, 0, 1, 4, 5, 6, 7):
         act_halo(n).start()
 
@@ -204,31 +208,23 @@
         ing_v[i] = stage[pl.ds(0, cin * nj)].astype(jnp.bfloat16).reshape(cin, nj, LANES)
         pltpu.make_async_copy(ing_v.at[i], ing_hbm.at[:, i], out_sem.at[ni + i]).start()
 
-    def to_core():
+    def to_group(q):
+        d, flip = lax.div(q, 2), lax.rem(q, 2)
         return pltpu.make_async_remote_copy(
-            src_ref=slots.at[1 - core], dst_ref=near, send_sem=p1_send.at[0], recv_sem=p1_recv.at[0],
-            device_id=other_core, device_id_type=MESH)
-
-    def to_group(d):
-        return pltpu.make_async_remote_copy(
-            src_ref=sums.at[place_across(d)], dst_ref=parts.at[place],
-            send_sem=p2_send.at[d], recv_sem=p2_recv.at[d], device_id=across(d), device_id_type=MESH)
+            src_ref=slots.at[core + flip * (1 - 2 * core), place_across(d)], dst_ref=parts.at[core, place],
+            send_sem=p1_send.at[q], recv_sem=p1_recv.at[q], device_id=across(d, flip), device_id_type=MESH)
 
     def to_z(dz):
         return pltpu.make_async_remote_copy(
-            src_ref=lifted.at[z], dst_ref=lifted.at[z], send_sem=p3_send.at[dz], recv_sem=p3_recv.at[dz],
+            src_ref=lifted.at[z], dst_ref=lifted.at[z], send_sem=p2_send.at[dz], recv_sem=p2_recv.at[dz],
             device_id=along_z(dz), device_id_type=MESH)
 
-    def back_group(d):
+    def back_group(q):
         return pltpu.make_async_remote_copy(
-            src_ref=full.at[core, place], dst_ref=full.at[core, place], send_sem=p4_send.at[d], recv_sem=p4_recv.at[d],
-            device_id=across(d), device_id_type=MESH)
-
-    def back_core(d):
-        at = source_across(d)
-        return pltpu.make_async_remote_copy(
-            src_ref=full.at[core, at], dst_ref=full.at[core, at], send_sem=p5_send.at[d], recv_sem=p5_recv.at[d],
-            device_id=other_core, device_id_type=MESH)
+            src_ref=mine, dst_ref=full.at[core, place], send_sem=p3_send.at[q], recv_sem=p3_recv.at[q],
+            device_id=across(lax.div(q, 2), lax.rem(q, 2)), device_id_type=MESH)
+
+    own = pltpu.make_async_copy(mine, full.at[core, place], mine_sem.at[0])
 
     def each(low, high, do):
         def body(t, carry):
@@ -237,68 +233,64 @@
 
         lax.fori_loop(low, high, body, 0)
 
-    to_core().start()
+    peers = 2 * group
+    each(1, peers, lambda t: to_group(peers - t).start())
+    parts[core, place] = slots[core, place]
+    for n in range(2):
+        halo(og_e, n, ho_send, ho_recv).start()
     w_in.wait()
     w = w_v[...].astype(jnp.float32).reshape(9, 3, cin, cout)
     by_tap = jnp.concatenate([w[:, e].reshape(9 * cin, cout) for e in range(3)], axis=1)
     w_fwd[...] = by_tap.T.astype(jnp.bfloat16)
     w_bwd[...] = jnp.concatenate([w[n].reshape(3 * cin, cout) for n in range(9)], axis=1).astype(jnp.bfloat16)
-    to_core().wait_recv()
-    sums[...] = slots[core] + near[...]
-    each(1, group, lambda d: to_group(group - d).start())
-    for n in range(2):
-        halo(og_e, n, ho_send, ho_recv).start()
-    parts[place] = sums[place]
     each(0, 2, forward)
-    each(1, group, lambda d: to_group(d).wait_recv())
-    lifted[z] = jnp.sum(parts[...], axis=0)
+    each(1, peers, lambda q: to_group(q).wait_recv())
+    lifted[z] = jnp.sum(parts[...], axis=(0, 1))
     each(1, nz, lambda dz: to_z(dz).start())
     for n in range(2, 8):
         halo(og_e, n, ho_send, ho_recv).start()
     each(2, ni, forward)
     each(1, nz, lambda dz: to_z(dz).wait_recv())
-    full[core, place] = jnp.sum(lifted[...], axis=0) * jnp.float32(scale)
-    each(1, group, lambda d: back_group(d).start())
-    back_core(0).start()
+    mine[...] = jnp.sum(lifted[...], axis=0) * jnp.float32(scale)
+    each(1, peers, lambda t: back_group(peers - t).start())
+    own.start()
     for n in range(8):
         halo(og_e, n, ho_send, ho_recv).wait_recv()
     each(0, ni, backward)
 
-    def forward_core(t):
-        d = t + 1
-        back_group(d).wait_recv()
-        back_core(d).start()
-
-    each(0, group - 1, forward_core)
-    each(0, group, lambda d: back_core(d).wait_recv())
+
+    for n in range(8):
+        act_halo(n).wait_send()
+        halo(og_e, n, ho_send, ho_recv).wait_send()
+    each(1, peers, lambda q: to_group(q).wait_send())
+    each(1, nz, lambda dz: to_z(dz).wait_send())
+    each(1, peers, lambda q: back_group(q).wait_send())
+    each(0, ni, lambda i: pltpu.make_async_copy(out_v.at[i], out_hbm.at[:, i], out_sem.at[i]).wait())
+    each(0, ni, lambda i: pltpu.make_async_copy(ing_v.at[i], ing_hbm.at[:, i], out_sem.at[ni + i]).wait())
+    own.wait()
+    each(1, peers, lambda q: back_group(q).wait_recv())
+
+
+def deliver(cin, cout, out_v, ing_v, full, out_hbm, ing_hbm, kg_hbm, dense, kg_v, sem):
+    copies = [
+        pltpu.make_async_copy(source, target, sem.at[n])
+        for n, (source, target) in enumerate(((out_v, out_hbm), (ing_v, ing_hbm), (kg_v, kg_hbm)))
+    ]
+    copies[0].start()
+    copies[1].start()
+    _, group, part, _ = full.shape
+    tall = 9 * cin
+    half = tall // 2
     for s in range(2 * group):
         dense[pl.ds(s * part, part)] = full[s // group, s % group]
     for n in range(9):
         rows = pl.ds(n * cin, cin)
-        kg_ref[pl.ds(n * 3 * cin, cin)] = dense[rows, pl.ds(0, cout)]
-        kg_ref[pl.ds((n * 3 + 1) * cin, cin)] = dense[rows, pl.ds(cout, cout)]
+        kg_v[pl.ds(n * 3 * cin, cin)] = dense[rows, pl.ds(0, cout)]
+        kg_v[pl.ds((n * 3 + 1) * cin, cin)] = dense[rows, pl.ds(cout, cout)]
     third = jnp.concatenate([dense[pl.ds(tall, half), :cout], dense[pl.ds(tall, half), cout:]], axis=0)
     for n in range(9):
-        kg_ref[pl.ds((n * 3 + 2) * cin, cin)] = third[n * cin : (n + 1) * cin]
-
-    for n in range(8):
-        act_halo(n).wait_send()
-        halo(og_e, n, ho_send, ho_recv).wait_send()
-    to_core().wait_send()
-    each(1, group, lambda d: to_group(d).wait_send())
-    each(1, nz, lambda dz: to_z(dz).wait_send())
-    each(1, group, lambda d: back_group(d).wait_send())
-    each(0, group, lambda d: back_core(d).wait_send())
-    each(0, ni, lambda i: pltpu.make_async_copy(out_v.at[i], out_hbm.at[:, i], out_sem.at[i]).wait())
-    each(0, ni, lambda i: pltpu.make_async_copy(ing_v.at[i], ing_hbm.at[:, i], out_sem.at[ni + i]).wait())
-
-
-def deliver(*refs):
-    count = len(refs) // 2
-    sem = refs[-1]
-    copies = [pltpu.make_async_copy(refs[n], refs[count + n], sem.at[n]) for n in range(count)]
-    for copy in copies:
-        copy.start()
+        kg_v[pl.ds((n * 3 + 2) * cin, cin)] = third[n * cin : (n + 1) * cin]
+    copies[2].start()
     for copy in copies:
         copy.wait()
 
@@ -313,12 +305,12 @@
     bf16, f32 = jnp.bfloat16, jnp.float32
     dma = pltpu.SemaphoreType.DMA
     taps = weights.transpose(2, 3, 4, 1, 0).reshape(27 * cin, cout)
-    output, in_grad, kernel_grad = pl.pallas_call(
+    output, in_grad, gathered = pl.pallas_call(
         functools.partial(kernel, sizes, scale),
         out_shape=(
             jax.ShapeDtypeStruct((cout, ni, nj, nk), bf16),
             jax.ShapeDtypeStruct((cin, ni, nj, nk), bf16),
-            jax.ShapeDtypeStruct((27 * cin, cout), f32),
+            jax.ShapeDtypeStruct((2, group, part, LANES), f32),
         ),
         in_specs=[
             pl.BlockSpec(memory_space=pltpu.HBM),
@@ -328,7 +320,7 @@
         out_specs=(
             pl.BlockSpec(memory_space=pl.ANY),
             pl.BlockSpec(memory_space=pl.ANY),
-            pl.BlockSpec(memory_space=pltpu.VMEM),
+            pl.BlockSpec(memory_space=pl.ANY),
         ),
         scratch_shapes=[
             pltpu.VMEM((cin, ni, nj, nk), bf16),
@@ -346,34 +338,39 @@
             pltpu.VMEM((9 * cin, 3 * cout), f32),
             pltpu.VMEM((2 * group * part, LANES), f32),
             pltpu.VMEM((2, group, part, LANES), f32),
-            pltpu.VMEM((group, part, LANES), f32),
-            pltpu.VMEM((group, part, LANES), f32),
-            pltpu.VMEM((group, part, LANES), f32),
+            pltpu.VMEM((2, group, part, LANES), f32),
             pltpu.VMEM((nz, part, LANES), f32),
-            pltpu.VMEM((2, group, part, LANES), f32),
+            pltpu.VMEM((part, LANES), f32),
             pltpu.VMEM((ni, cout, nj, nk), bf16),
             pltpu.VMEM((ni, cin, nj, nk), bf16),
             dma((3,)),
             dma((2 * ni,)),
             dma((8,)), dma((8,)), dma((8,)), dma((8,)),
-            dma((1,)), dma((1,)),
-            dma((group,)), dma((group,)),
+            dma((2 * group,)), dma((2 * group,)),
             dma((nz,)), dma((nz,)),
-            dma((group,)), dma((group,)),
-            dma((group,)), dma((group,)),
+            dma((2 * group,)), dma((2 * group,)),
+            dma((1,)),
         ],
         compiler_params=pltpu.CompilerParams(
             collective_id=0, has_side_effects=True, vmem_limit_bytes=48 * 1024 * 1024
         ),
         cost_estimate=pl.CostEstimate(flops=3_000_000_000, bytes_accessed=4_000_000, transcendentals=0),
     )(*(pltpu.with_memory_space_constraint(x, pltpu.HBM) for x in (activations[0], taps, out_grad[0])))
-    held = tuple(pltpu.with_memory_space_constraint(x, pltpu.VMEM) for x in (output, in_grad, kernel_grad))
+    held = tuple(pltpu.with_memory_space_constraint(x, pltpu.VMEM) for x in (output, in_grad, gathered))
     output, in_grad, kernel_grad = pl.pallas_call(
-        deliver,
-        out_shape=tuple(jax.ShapeDtypeStruct(x.shape, x.dtype) for x in held),
+        functools.partial(deliver, cin, cout),
+        out_shape=(
+            jax.ShapeDtypeStruct(output.shape, bf16),
+            jax.ShapeDtypeStruct(in_grad.shape, bf16),
+            jax.ShapeDtypeStruct((27 * cin, cout), f32),
+        ),
         in_specs=[pl.BlockSpec(memory_space=pltpu.VMEM)] * 3,
         out_specs=(pl.BlockSpec(memory_space=pltpu.HBM),) * 3,
-        scratch_shapes=[dma((3,))],
+        scratch_shapes=[
+            pltpu.VMEM((2 * group * part, LANES), f32),
+            pltpu.VMEM((27 * cin, cout), f32),
+            dma((3,)),
+        ],
     )(*held)
     kernel_grad = kernel_grad.reshape(3, 3, 3, cin, cout).transpose(4, 3, 0, 1, 2)
     return (output[None], in_grad[None], kernel_grad)

time: 37.5 us -> 36.3 us (0.968)
  Pallas kernels: 36.8 us -> 35.5 us
    pallas_call x1, Pallas kernels: 35.5 us -> 34.2 us  [local(): pl.pallas_call(functools.partial(kernel, sizes, scale), out_shape=(jax.Sh...]
where the time goes in v4:
time: 36.3 us; the launch traced here: 36.2 us
  Pallas kernels  35.5 us (98%)
  between operations  0.64 us (2%)
    pallas_call x1, Pallas kernels, local(): pl.pallas_call(functools.partial(kernel, sizes, scale), out_shape=(jax.Sh...  34.2 us
    pallas_call x1, Pallas kernels, local(): pl.pallas_call(functools.partial(deliver, cin, cout), out_shape=(jax.Shap...  1.31 us

profile of v4, /device:TPU:1, one launch (start us, length us, event | category | flops | bytes accessed | tf_op | source)
XLA Modules:
  0.0 36.2 jit_solution(17288613239894004310)
XLA Ops:
  0.6 34.2 %shard_map.58 = (bf16[64,4,16,128]{3,2,1,0:T(8,128)(2,1)S(1)}, bf16[32,4,16,128]{3,2,1,0:T(8,128)(2,1)S(1)}, f32[2,16,14,128]{3,2,1,0:T(8,128)S(1)}) custom-call(bf16[32,4,16,128]{3,2,1,0:T(8,128)(2,1)} %bitcast.12, bf16[864,64]{1,0:T(8,128)(2,1)} %bitcast.15, bf16[64,4,16,128]{3,2,1,0:T(8,128)(2,1)} %bitcast.10), custom_call_target="tpu_custom_call" | custom-call | flops 3000000000 | bytes 4000000 | tf_op jit(solution)/shard_map/pallas_call | solution.py:308
  34.9 1.3 %shard_map.59 = (bf16[64,4,16,128]{3,2,1,0:T(8,128)(2,1)}, bf16[32,4,16,128]{3,2,1,0:T(8,128)(2,1)}, f32[864,64]{1,0:T(8,128)}) custom-call(bf16[64,4,16,128]{3,2,1,0:T(8,128)(2,1)S(1)} %get-tuple-element.9.out_v, bf16[32,4,16,128]{3,2,1,0:T(8,128)(2,1)S(1)} %get-tuple-element.10.ing_v, f32[2,16,14,128]{3,2,1,0:T(8,128)S(1)} %get-tuple-element.11.full), custom_call_target="tpu_custom_call" | custom-call | tf_op jit(solution)/shard_map/pallas_call | solution.py:360

commit v5 on v4

--- a/solution.py
+++ b/solution.py
@@ -16,7 +16,7 @@
 def kernel(sizes, scale, act_hbm, w_hbm, og_hbm, out_hbm, ing_hbm, full,
            act_v, w_v, og_v, act_e, og_e, og_r, land_x, land_y, land_c, stage, w_fwd, w_bwd, grad, dense, slots, parts, lifted, mine,
            out_v, ing_v, in_sem, out_sem, ha_send, ha_recv, ho_send, ho_recv,
-           p1_send, p1_recv, p2_send, p2_recv, p3_send, p3_recv, mine_sem):
+           p1_send, p1_recv, p2_send, p2_recv, p3_send, p3_recv, mine_sem, seen):
     n_dp, n_gx, n_gy = sizes
     cin, ni, nj, _ = act_v.shape
     cout = og_v.shape[0]
@@ -30,17 +30,17 @@
         return (dp, lax.rem(gx + di + n_gx, n_gx), lax.rem(gy + dj + n_gy, n_gy))
 
     def along_z(dz):
-        return (dp, lax.rem(z + dz, nz) * 2 + core, gy)
+        return (dp, lax.rem(z + dz + nz, nz) * 2 + core, gy)
 
     def across(d, flip=0):
         return (
-            lax.rem(dp + lax.div(d, n_gy), n_dp),
+            lax.rem(dp + d // n_gy, n_dp),
             z * 2 + core + flip * (1 - 2 * core),
-            lax.rem(gy + lax.rem(d, n_gy), n_gy),
+            lax.rem(gy + d % n_gy, n_gy),
         )
 
     def place_across(d):
-        return lax.rem(dp + lax.div(d, n_gy), n_dp) * n_gy + lax.rem(gy + lax.rem(d, n_gy), n_gy)
+        return lax.rem(dp + d // n_gy, n_dp) * n_gy + lax.rem(gy + d % n_gy, n_gy)
 
     act_in = pltpu.make_async_copy(act_hbm, act_v, in_sem.at[0])
     og_in = pltpu.make_async_copy(og_hbm, og_v, in_sem.at[1])
@@ -54,16 +54,21 @@
     def greet(target):
         pl.semaphore_signal(barrier, inc=1, device_id=target, device_id_type=MESH)
 
-    steps = [(d, flip) for d in range(2, group) for flip in range(2) if d not in (n_gy - 1,)]
-    hops = {}
-    for d, flip in steps:
-        far_x, far_y = 2 * (d // n_gy), d % n_gy
-        hops[d, flip] = min(far_y, n_gy - far_y) / 2 + (1.5 if far_y % 2 else far_x)
-    targets = [(hops[d, flip], across(d, flip)) for d, flip in steps]
-    targets += [(min(d, nz - d), along_z(d)) for d in range(1, nz)]
-    targets += [(abs(di) + 1.5 * abs(dj), shifted(di, dj)) for di, dj in AROUND]
-    for _, target in sorted(targets, key=lambda t: -t[0]):
+    def hops(d):
+        far_y = d % n_gy
+        return min(far_y, n_gy - far_y) / 2 + (1.5 if far_y % 2 else 2 * (d // n_gy))
+
+    peers = 2 * group
+    far_first = sorted(range(1, peers), key=lambda q: -hops(q // 2))
+    near = [(hops(d), across(d, flip)) for d in range(2, group) for flip in range(2) if d != n_gy - 1 and hops(d) <= 2]
+    near += [(d, along_z(way * d)) for d in range(1, min(nz, 3)) for way in (1, -1)]
+    near += [(abs(di) + 1.5 * abs(dj), shifted(di, dj)) for di, dj in AROUND]
+    for _, target in sorted(near, key=lambda t: -t[0]):
         greet(target)
+
+    def tell():
+        for target in (across(n_gy % group), across(n_gy // 2), along_z(2), along_z(-2)):
+            pl.semaphore_signal(seen, inc=1, device_id=target, device_id_type=MESH)
 
     def halo(field, n, send, recv, landing=None):
         di, dj = AROUND[n]
@@ -102,9 +107,10 @@
         return carry
 
     lax.fori_loop(0, ni, turn_act, 0)
-    pl.semaphore_wait(barrier, 8 + 2 * (group - 3) + (nz - 1))
-    for n in (2, 3, 0, 1, 4, 5, 6, 7):
+    pl.semaphore_wait(barrier, len(near))
+    for n in (4, 5, 6, 7, 2, 3, 0, 1):
         act_halo(n).start()
+    tell()
 
     og_in.wait()
 
@@ -163,13 +169,17 @@
             grad[pl.ds((3 * a + b) * cin, cin)] += term[a * cin : (a + 1) * cin]
     tall = 9 * cin
     half = tall // 2
-    dense[pl.ds(0, tall)] = grad[:, :LANES]
     dense[pl.ds(tall, half)] = jnp.concatenate([grad[:half, LANES:], grad[half:, LANES:]], axis=1)
     part = slots.shape[2]
     extra = 2 * group * part - tall - half
     if extra:
         dense[pl.ds(tall + half, extra)] = jnp.zeros((extra, LANES), jnp.float32)
     for s in range(2 * group):
+        if (s + 1) * part <= tall:
+            slots[s // group, s % group] = grad[pl.ds(s * part, part), pl.ds(0, LANES)]
+            continue
+        if s * part < tall:
+            dense[pl.ds(s * part, tall - s * part)] = grad[pl.ds(s * part, tall - s * part), pl.ds(0, LANES)]
         slots[s // group, s % group] = dense[pl.ds(s * part, part)]
 
     def forward(i):
@@ -209,7 +219,7 @@
         pltpu.make_async_copy(ing_v.at[i], ing_hbm.at[:, i], out_sem.at[ni + i]).start()
 
     def to_group(q):
-        d, flip = lax.div(q, 2), lax.rem(q, 2)
+        d, flip = q // 2, q % 2
         return pltpu.make_async_remote_copy(
             src_ref=slots.at[core + flip * (1 - 2 * core), place_across(d)], dst_ref=parts.at[core, place],
             send_sem=p1_send.at[q], recv_sem=p1_recv.at[q], device_id=across(d, flip), device_id_type=MESH)
@@ -222,7 +232,7 @@
     def back_group(q):
         return pltpu.make_async_remote_copy(
             src_ref=mine, dst_ref=full.at[core, place], send_sem=p3_send.at[q], recv_sem=p3_recv.at[q],
-            device_id=across(lax.div(q, 2), lax.rem(q, 2)), device_id_type=MESH)
+            device_id=across(q // 2, q % 2), device_id_type=MESH)
 
     own = pltpu.make_async_copy(mine, full.at[core, place], mine_sem.at[0])
 
@@ -233,8 +243,9 @@
 
         lax.fori_loop(low, high, body, 0)
 
-    peers = 2 * group
-    each(1, peers, lambda t: to_group(peers - t).start())
+    pl.semaphore_wait(seen, 4)
+    for q in far_first:
+        to_group(q).start()
     parts[core, place] = slots[core, place]
     for n in range(2):
         halo(og_e, n, ho_send, ho_recv).start()
@@ -252,7 +263,8 @@
     each(2, ni, forward)
     each(1, nz, lambda dz: to_z(dz).wait_recv())
     mine[...] = jnp.sum(lifted[...], axis=0) * jnp.float32(scale)
-    each(1, peers, lambda t: back_group(peers - t).start())
+    for q in far_first:
+        back_group(q).start()
     own.start()
     for n in range(8):
         halo(og_e, n, ho_send, ho_recv).wait_recv()
@@ -272,12 +284,15 @@
 
 
 def deliver(cin, cout, out_v, ing_v, full, out_hbm, ing_hbm, kg_hbm, dense, kg_v, sem):
+    piece = cin // 2
+    pairs = [(out_v, out_hbm, n) for n in range(0, cout, piece)] + [(ing_v, ing_hbm, n) for n in range(0, cin, piece)]
     copies = [
-        pltpu.make_async_copy(source, target, sem.at[n])
-        for n, (source, target) in enumerate(((out_v, out_hbm), (ing_v, ing_hbm), (kg_v, kg_hbm)))
+        pltpu.make_async_copy(source.at[pl.ds(n, piece)], target.at[pl.ds(n, piece)], sem.at[m])
+        for m, (source, target, n) in enumerate(pairs)
     ]
-    copies[0].start()
-    copies[1].start()
+    for copy in copies:
+        copy.start()
+    last = pltpu.make_async_copy(kg_v, kg_hbm, sem.at[len(pairs)])
     _, group, part, _ = full.shape
     tall = 9 * cin
     half = tall // 2
@@ -290,9 +305,10 @@
     third = jnp.concatenate([dense[pl.ds(tall, half), :cout], dense[pl.ds(tall, half), cout:]], axis=0)
     for n in range(9):
         kg_v[pl.ds((n * 3 + 2) * cin, cin)] = third[n * cin : (n + 1) * cin]
-    copies[2].start()
+    last.start()
     for copy in copies:
         copy.wait()
+    last.wait()
 
 
 def local(sizes, activations, weights, out_grad):
@@ -350,6 +366,7 @@
             dma((nz,)), dma((nz,)),
             dma((2 * group,)), dma((2 * group,)),
             dma((1,)),
+            pltpu.SemaphoreType.REGULAR,
         ],
         compiler_params=pltpu.CompilerParams(
             collective_id=0, has_side_effects=True, vmem_limit_bytes=48 * 1024 * 1024
@@ -369,7 +386,7 @@
         scratch_shapes=[
             pltpu.VMEM((2 * group * part, LANES), f32),
             pltpu.VMEM((27 * cin, cout), f32),
-            dma((3,)),
+            dma((2 * cout // cin + 3,)),
         ],
     )(*held)
     kernel_grad = kernel_grad.reshape(3, 3, 3, cin, cout).transpose(4, 3, 0, 1, 2)

time: 36.3 us -> 35.5 us (0.978)
  Pallas kernels: 35.5 us -> 34.7 us
    pallas_call x1, Pallas kernels: 34.2 us -> 33.4 us  [local(): pl.pallas_call(functools.partial(kernel, sizes, scale), out_shape=(jax.Sh...]
where the time goes in v5:
time: 35.5 us; the launch traced here: 35.4 us
  Pallas kernels  34.7 us (98%)
  between operations  0.64 us (2%)
    pallas_call x1, Pallas kernels, local(): pl.pallas_call(functools.partial(kernel, sizes, scale), out_shape=(jax.Sh...  33.4 us
    pallas_call x1, Pallas kernels, local(): pl.pallas_call(functools.partial(deliver, cin, cout), out_shape=(jax.Shap...  1.35 us

profile of v5, /device:TPU:1, one launch (start us, length us, event | category | flops | bytes accessed | tf_op | source)
XLA Modules:
  0.0 35.4 jit_solution(2561878868611973422)
XLA Ops:
  0.6 33.4 %shard_map.58 = (bf16[64,4,16,128]{3,2,1,0:T(8,128)(2,1)S(1)}, bf16[32,4,16,128]{3,2,1,0:T(8,128)(2,1)S(1)}, f32[2,16,14,128]{3,2,1,0:T(8,128)S(1)}) custom-call(bf16[32,4,16,128]{3,2,1,0:T(8,128)(2,1)} %bitcast.12, bf16[864,64]{1,0:T(8,128)(2,1)} %bitcast.15, bf16[64,4,16,128]{3,2,1,0:T(8,128)(2,1)} %bitcast.10), custom_call_target="tpu_custom_call" | custom-call | flops 3000000000 | bytes 4000000 | tf_op jit(solution)/shard_map/pallas_call | solution.py:324
  34.0 1.3 %shard_map.59 = (bf16[64,4,16,128]{3,2,1,0:T(8,128)(2,1)}, bf16[32,4,16,128]{3,2,1,0:T(8,128)(2,1)}, f32[864,64]{1,0:T(8,128)}) custom-call(bf16[64,4,16,128]{3,2,1,0:T(8,128)(2,1)S(1)} %get-tuple-element.9.out_v, bf16[32,4,16,128]{3,2,1,0:T(8,128)(2,1)S(1)} %get-tuple-element.10.ing_v, f32[2,16,14,128]{3,2,1,0:T(8,128)S(1)} %get-tuple-element.11.full), custom_call_target="tpu_custom_call" | custom-call | tf_op jit(solution)/shard_map/pallas_call | solution.py:377

commit v6 on v5

--- a/solution.py
+++ b/solution.py
@@ -108,9 +108,9 @@
 
     lax.fori_loop(0, ni, turn_act, 0)
     pl.semaphore_wait(barrier, len(near))
+    tell()
     for n in (4, 5, 6, 7, 2, 3, 0, 1):
         act_halo(n).start()
-    tell()
 
     og_in.wait()
 
@@ -255,13 +255,16 @@
     w_fwd[...] = by_tap.T.astype(jnp.bfloat16)
     w_bwd[...] = jnp.concatenate([w[n].reshape(3 * cin, cout) for n in range(9)], axis=1).astype(jnp.bfloat16)
     each(0, 2, forward)
-    each(1, peers, lambda q: to_group(q).wait_recv())
+    for q in reversed(far_first):
+        to_group(q).wait_recv()
     lifted[z] = jnp.sum(parts[...], axis=(0, 1))
-    each(1, nz, lambda dz: to_z(dz).start())
+    for dz in sorted(range(1, nz), key=lambda d: -min(d, nz - d)):
+        to_z(dz).start()
     for n in range(2, 8):
         halo(og_e, n, ho_send, ho_recv).start()
     each(2, ni, forward)
-    each(1, nz, lambda dz: to_z(dz).wait_recv())
+    for dz in sorted(range(1, nz), key=lambda d: min(d, nz - d)):
+        to_z(dz).wait_recv()
     mine[...] = jnp.sum(lifted[...], axis=0) * jnp.float32(scale)
     for q in far_first:
         back_group(q).start()
@@ -280,7 +283,8 @@
     each(0, ni, lambda i: pltpu.make_async_copy(out_v.at[i], out_hbm.at[:, i], out_sem.at[i]).wait())
     each(0, ni, lambda i: pltpu.make_async_copy(ing_v.at[i], ing_hbm.at[:, i], out_sem.at[ni + i]).wait())
     own.wait()
-    each(1, peers, lambda q: back_group(q).wait_recv())
+    for q in reversed(far_first):
+        back_group(q).wait_recv()
 
 
 def deliver(cin, cout, out_v, ing_v, full, out_hbm, ing_hbm, kg_hbm, dense, kg_v, sem):

time: 35.5 us -> 35.2 us (level)
  no operation moved by 1% of the time
where the time goes in v6:
time: 35.2 us; the launch traced here: 35.1 us
  Pallas kernels  34.5 us (98%)
  between operations  0.64 us (2%)
    pallas_call x1, Pallas kernels, local(): pl.pallas_call(functools.partial(kernel, sizes, scale), out_shape=(jax.Sh...  33.1 us
    pallas_call x1, Pallas kernels, local(): pl.pallas_call(functools.partial(deliver, cin, cout), out_shape=(jax.Shap...  1.35 us

profile of v6, /device:TPU:1, one launch (start us, length us, event | category | flops | bytes accessed | tf_op | source)
XLA Modules:
  0.0 35.1 jit_solution(13167014039715232828)
XLA Ops:
  0.6 33.1 %shard_map.58 = (bf16[64,4,16,128]{3,2,1,0:T(8,128)(2,1)S(1)}, bf16[32,4,16,128]{3,2,1,0:T(8,128)(2,1)S(1)}, f32[2,16,14,128]{3,2,1,0:T(8,128)S(1)}) custom-call(bf16[32,4,16,128]{3,2,1,0:T(8,128)(2,1)} %bitcast.12, bf16[864,64]{1,0:T(8,128)(2,1)} %bitcast.15, bf16[64,4,16,128]{3,2,1,0:T(8,128)(2,1)} %bitcast.10), custom_call_target="tpu_custom_call" | custom-call | flops 3000000000 | bytes 4000000 | tf_op jit(solution)/shard_map/pallas_call | solution.py:328
  33.8 1.3 %shard_map.59 = (bf16[64,4,16,128]{3,2,1,0:T(8,128)(2,1)}, bf16[32,4,16,128]{3,2,1,0:T(8,128)(2,1)}, f32[864,64]{1,0:T(8,128)}) custom-call(bf16[64,4,16,128]{3,2,1,0:T(8,128)(2,1)S(1)} %get-tuple-element.9.out_v, bf16[32,4,16,128]{3,2,1,0:T(8,128)(2,1)S(1)} %get-tuple-element.10.ing_v, f32[2,16,14,128]{3,2,1,0:T(8,128)S(1)} %get-tuple-element.11.full), custom_call_target="tpu_custom_call" | custom-call | tf_op jit(solution)/shard_map/pallas_call | solution.py:381
